TPU v7x, 256 devices: a whole 4x4x8 slice. The times are simulated.
256 devices in a mesh: date: 128 (over y, x, z), band: 2 (over core).
Axes of the slice: x: 4, y: 4, z: 8, core: 2. Of those that a mesh axis runs over, the one named last changes fastest.
Arguments:
- observations: float32 [8192, 8, 512], P('date', 'band'), may hold values from -6 to 6
- valid: int32 [8192, 512], P('date'), may hold values 0 or 1
- breaks: int32 [8192, 512], P('date'), may hold values 0 or 1
- refit: int32 [128, 4], P('date'), may hold values from 0 to 63, as said below
Outputs:
- coefs: float32 [128, 4, 8, 8, 512], P('date', None, 'band')
- spread: float32 [128, 4, 512], P('date')
Inputs may be any that keep to these rules, and one draw needn't show every extreme that they name: `refit`: each row holds 4 different dates in increasing order.
All inputs are finite; a program needn't handle non-finite values. No bound on the sum of `valid` or of `breaks` on one device may be relied on, other than what follows from the above.
Results may differ from a plain program's by a relative error of at most 0.0003.
Values sent between devices are 32-bit elements; how exact they have to be, the bound alone decides.
A program may use at most 64 MiB of HBM per device.

v0:
```python
import math

import jax
import jax.numpy as jnp
from jax import lax
from jax.sharding import Mesh
from jax.sharding import PartitionSpec as P

DATE = ("date_0", "date_1", "date_2")


ridge_weight = 1.0
year_period = 365.25
upper_pairs = [(i, j) for i in range(8) for j in range(i, 8)]


def filled_with(value, identity):
    return jax.tree.map(
        lambda part, zero: jnp.zeros_like(part) + jnp.asarray(zero, part.dtype), value, identity
    )


def all_in_one(value, axis):
    leaves = jax.tree.leaves(value)
    order = sorted(range(len(leaves)), key=lambda k: -leaves[k].size)
    width = (1, *leaves[order[0]].shape)[-1]
    lines = [
        jnp.pad(leaves[k].reshape(-1), (0, -leaves[k].size % width)).reshape(-1, width)
        for k in order
    ]
    both, at, found = (lax.all_gather(jnp.concatenate(lines), axis), 0, {})
    for k, line in zip(order, lines):
        piece = both[:, at : at + len(line)].reshape(len(both), -1)
        found[k] = piece[:, : leaves[k].size].reshape(-1, *leaves[k].shape)
        at += len(line)
    numbers = iter(range(len(leaves)))
    return jax.tree.map(lambda _: found[next(numbers)], value)


def prefix_by_axis(value, axes, combine, identity):
    before = start = filled_with(value, identity)
    running = value
    for axis in reversed(axes):
        devices, mine = (lax.axis_size(axis), lax.axis_index(axis))
        pieces = all_in_one(running, axis)
        inside, running = (start, start)
        for k in range(devices):
            passed = k < mine
            running = combine(running, jax.tree.map(lambda part: part[k], pieces))
            inside = jax.tree.map(lambda new, old: jnp.where(passed, new, old), running, inside)
        before = combine(inside, before)
    return before


def laid_out(blocks, dim):
    blocks = jnp.moveaxis(blocks, 0, dim)
    shape = blocks.shape
    return blocks.reshape(*shape[:dim], shape[dim] * shape[dim + 1], *shape[dim + 2 :])


def sent_to_all(value, axis):
    devices = lax.axis_size(axis)
    return lax.all_to_all(
        jnp.broadcast_to(value[None], (devices, *value.shape)), axis, 0, 0, tiled=True
    )


def gathered_copies(value, axis, dim):
    return laid_out(sent_to_all(value, axis), dim)


def of_everyone(value, axis):
    everything = sent_to_all(value, axis)
    return jnp.sum(everything, axis=0)


def harmonics(first, length, total_dates):
    moment = (first + jnp.arange(length, dtype=jnp.int32)).astype(jnp.float32)
    scaled = 2.0 * (moment + 0.5) / total_dates - 1.0
    phase = 2.0 * math.pi * moment / year_period
    design = [jnp.ones_like(moment), scaled]
    for k in range(1, 4):
        design.append(jnp.cos(k * phase))
        design.append(jnp.sin(k * phase))
    return jnp.stack(design)


def window_weights(valid, breaks, picks):
    length = valid.shape[0]
    segment_id = jnp.cumsum(breaks, axis=0)
    rows_at = jnp.concatenate([picks, jnp.array([length - 1], jnp.int32)])
    seg_at = jnp.take(segment_id, rows_at, axis=0)
    places = jnp.arange(length, dtype=jnp.int32)
    inside = (places[None, :, None] <= rows_at[:, None, None]) & (
        segment_id[None] == seg_at[:, None, :]
    )
    weight = jnp.where(inside, valid[None].astype(jnp.float32), jnp.float32(0.0))
    opened = (seg_at == 0).astype(jnp.float32)
    reset_flag = (segment_id[-1] > 0).astype(jnp.float32)
    return (weight, opened, reset_flag)


def window_pieces(series, clear, starts, picks, first, total_dates, band_slot, share):
    hi = lax.Precision.HIGHEST
    length = series.shape[0]
    design = harmonics(first, length, total_dates)
    table = jnp.stack([design[i] * design[j] for i, j in upper_pairs])
    table = lax.dynamic_slice_in_dim(table, band_slot * share, share, 0)
    weight, opened, reset_flag = window_weights(clear, starts, picks)
    gram_sum = jnp.einsum("rtp,kt->rkp", weight, table, precision=hi)
    parts = []
    for b in range(series.shape[1]):
        parts.append(
            jnp.einsum("rtp,it->rip", weight * series[:, b, :][None], design, precision=hi)
        )
    moments = jnp.stack(parts, axis=1)
    sum_sq = jnp.einsum("rtp,tbp->rbp", weight, series * series, precision=hi)
    counts = jnp.sum(weight, axis=1)
    return (gram_sum, moments, sum_sq, counts, opened, reset_flag)


def refit_model(gram_sum, moments, sum_sq):
    entry = [[None] * 8 for _ in range(8)]
    for n, (i, j) in enumerate(upper_pairs):
        entry[i][j] = gram_sum[:, n]
        entry[j][i] = gram_sum[:, n]
    lower = [[None] * 8 for _ in range(8)]
    for j in range(8):
        diag = entry[j][j] + ridge_weight
        for k in range(j):
            diag = diag - lower[j][k] * lower[j][k]
        lower[j][j] = jnp.sqrt(diag)
        for i in range(j + 1, 8):
            value = entry[i][j]
            for k in range(j):
                value = value - lower[i][k] * lower[j][k]
            lower[i][j] = value / lower[j][j]
    rhs = [moments[:, :, i] for i in range(8)]
    forward = []
    for i in range(8):
        value = rhs[i]
        for k in range(i):
            value = value - lower[i][k][:, None] * forward[k]
        forward.append(value / lower[i][i][:, None])
    solved = [None] * 8
    for i in reversed(range(8)):
        value = forward[i]
        for k in range(i + 1, 8):
            value = value - lower[k][i][:, None] * solved[k]
        solved[i] = value / lower[i][i][:, None]
    resid = sum_sq
    for i in range(8):
        applied = entry[i][0][:, None] * solved[0]
        for j in range(1, 8):
            applied = applied + entry[i][j][:, None] * solved[j]
        resid = resid - solved[i] * (2.0 * rhs[i] - applied)
    return (jnp.stack(solved, axis=2), jnp.sum(resid, axis=1))


def join_states(earlier, later):
    keep = later[0] > 0.5
    wider = keep[..., None, :]
    return (
        jnp.maximum(earlier[0], later[0]),
        jnp.where(wider, later[1], earlier[1] + later[1]),
        jnp.where(wider, later[2], earlier[2] + later[2]),
        jnp.where(wider, later[3], earlier[3] + later[3]),
        jnp.where(keep, later[4], earlier[4] + later[4]),
    )


def per_device(observations, valid, breaks, refit):
    length = observations.shape[0]
    nbands = observations.shape[1]
    pixels = observations.shape[2]
    picks_n = refit.shape[1]
    windows_all = lax.axis_size(DATE)
    total_dates = windows_all * length
    share = 36
    band_slot = 0
    share = 36 // lax.axis_size("band")
    band_slot = lax.axis_index("band")
    window = lax.axis_index(DATE)
    gram_sum, moments, sum_sq, counts, opened, reset_flag = window_pieces(
        observations, valid, breaks, refit[0], window * length, total_dates, band_slot, share
    )
    ending = (
        reset_flag,
        gram_sum[picks_n],
        moments[picks_n].reshape(nbands * 8, pixels),
        sum_sq[picks_n],
        counts[picks_n],
    )
    blank = (
        jnp.zeros_like(ending[0]),
        jnp.zeros_like(ending[1]),
        jnp.zeros_like(ending[2]),
        jnp.zeros_like(ending[3]),
        jnp.zeros_like(ending[4]),
    )
    carried = prefix_by_axis(ending, DATE, join_states, blank)
    head = opened[:picks_n]
    gram_at = gram_sum[:picks_n] + head[:, None] * carried[1][None]
    mom_at = moments[:picks_n] + head[:, None, None] * carried[2].reshape(nbands, 8, pixels)[None]
    sq_at = sum_sq[:picks_n] + head[:, None] * carried[3][None]
    cnt_at = counts[:picks_n] + head * carried[4][None]
    gram_at = gathered_copies(gram_at, "band", 1)
    coefs, resid = refit_model(gram_at, mom_at, sq_at)
    total_resid = of_everyone(resid, "band")
    spread = total_resid / jnp.maximum(cnt_at, 1.0)
    return (coefs[None], spread[None])


def solution(mesh):
    split = Mesh(
        mesh.devices.reshape(4, 4, 8, mesh.shape["band"]), ("date_0", "date_1", "date_2", "band")
    )
    placed = (P(DATE, "band", None), P(DATE, None), P(DATE, None), P(DATE, None))
    return jax.shard_map(
        per_device,
        mesh=split,
        in_specs=placed,
        out_specs=(P(DATE, None, "band", None, None), P(DATE, None, None)),
        check_vma=False,
    )
```

profile of v0, /device:TPU:25, one launch (start us, length us, event | category | flops | bytes accessed | tf_op | source)
XLA Modules:
  0.0 118.0 jit_solution(5207002057228329717)
XLA Ops:
  0.7 0.8 compare_and_fusion.2
  1.5 0.7 pad_add_fusion
  2.8 0.6 fusion.165
  5.9 0.6 fusion.151
  6.5 0.6 fusion.159
  8.4 0.6 fusion.147
  11.4 0.6 fusion.157
  12.0 0.6 fusion.171
  13.2 1.0 reduce_window_sum.11
  15.0 0.7 fusion.131
  17.1 1.3 %mul.2928 = f32[64,4,512]{2,1,0:T(4,128)S(1)} multiply(f32[64,4,512]{2,1,0:T(4,128)} %param.5, f32[64,4,512]{2,1,0:T(4,128)} %param.5) | non-fusion elementwise | flops 131072 | bytes 1572864 | tf_op jit(solution)/shard_map/mul | solution.py:117
  18.5 1.0 fusion.179
  20.2 5.5 %fusion = f32[512,4,5]{2,1,0:T(4,128)S(1)} fusion(f32[64,4,512]{0,1,2:T(4,128)S(1)} %copy.105, f32[64,512]{0,1:T(8,128)S(1)} %copy.91, s32[5,512]{0,1:T(8,128)S(1)} %copy.90, s32[64,512]{0,1:T(8,128)S(1)} %copy.89, pred[5,64]{1,0:T(8,128)(4,1)S(1)} %iota_compare_fusion), kind=kOutput, calls=%fused_computation.2 | convolution fusion | flops 8355840 | bytes 837952 | tf_op jit(solution)/shard_map/rtp,tbp->rbp/dot_general | solution.py:117
  26.7 1.0 copy.133
  27.7 0.9 copy.135
  28.6 0.9 copy.134
  29.5 0.8 copy.136
  30.3 5.5 %select_reduce_fusion = (f32[5,512]{0,1:T(8,128)S(1)}, f32[5,64,512]{1,0,2:T(8,128)}, f32[5,64,512]{1,0,2:T(8,128)}, f32[5,64,512]{1,0,2:T(8,128)}, f32[5,64,512]{1,0,2:T(8,128)}, /*index=5*/f32[5,64,512]{1,0,2:T(8,128)S(1)}) fusion(f32[64,512]{0,1:T(8,128)S(1)} %copy.91, s32[5,512]{0,1:T(8,128)S(1)} %copy.90, s32[64,512]{0,1:T(8,128)S(1)} %copy.89, ...), kind=kLoop, calls=%fused_computation.1 | loop fusion | flops 1308160 | bytes 4084032 | tf_op jit(solution)/shard_map/reduce_sum | solution.py:118
  36.0 3.0 %fusion.25 = f32[5,1,8,512]{3,2,0,1:T(8,128)S(1)} fusion(f32[5,64,512]{1,0,2:T(8,128)} %get-tuple-element.102, f32[8,64]{1,0:T(8,128)S(1)} %stack.16), kind=kOutput, calls=%fused_computation.24 | convolution fusion | flops 15728640 | bytes 739328 | tf_op jit(solution)/shard_map/rtp,it->rip/dot_general | solution.py:114
  39.3 2.9 %fusion.22 = f32[5,1,8,512]{3,2,0,1:T(8,128)S(1)} fusion(f32[5,64,512]{1,0,2:T(8,128)} %get-tuple-element.103, f32[8,64]{1,0:T(8,128)S(1)} %stack.16), kind=kOutput, calls=%fused_computation.23 | convolution fusion | flops 15728640 | bytes 739328 | tf_op jit(solution)/shard_map/rtp,it->rip/dot_general | solution.py:114
  42.2 1.3 %fusion.19 = f32[5,1,8,512]{3,2,0,1:T(8,128)S(1)} fusion(f32[5,64,512]{1,0,2:T(8,128)S(1)} %copy-done.1, f32[8,64]{1,0:T(8,128)S(1)} %stack.16), kind=kOutput, calls=%fused_computation.22 | convolution fusion | flops 15728640 | bytes 739328 | tf_op jit(solution)/shard_map/rtp,it->rip/dot_general | solution.py:114
  43.5 1.3 %fusion.16 = f32[5,1,8,512]{3,2,0,1:T(8,128)S(1)} fusion(f32[5,64,512]{1,0,2:T(8,128)S(1)} %copy-done, f32[8,64]{1,0:T(8,128)S(1)} %stack.16), kind=kOutput, calls=%fused_computation.21 | convolution fusion | flops 15728640 | bytes 739328 | tf_op jit(solution)/shard_map/rtp,it->rip/dot_general | solution.py:114
  45.2 1.3 %fusion.13 = f32[5,18,512]{2,1,0:T(8,128)S(1)} fusion(f32[5,64,512]{1,0,2:T(8,128)S(1)} %get-tuple-element.106, f32[36,64]{1,0:T(8,128)S(1)} %stack.22, s32[]{:T(128)S(6)} %select_n.1259), kind=kOutput, calls=%fused_computation.20 | convolution fusion | flops 35389440 | bytes 2293764 | tf_op jit(solution)/shard_map/rtp,kt->rkp/dot_general | solution.py:110
  46.8 24.2 %all-gather = f32[448,512]{1,0:T(8,128)S(1)} all-gather(f32[56,512]{1,0:T(8,128)S(1)} %concatenate.43), channel_id=2, replica_groups=mesh['date_0'=4,'date_1'=4,'date_2'=8,'band'=2] {'date_2'}, dimensions={0}, use_global_device_ids=true | all-gather | bytes 1032192 | tf_op jit(solution)/shard_map/all_gather | solution.py:31
  71.4 10.6 %all-gather.1 = f32[224,512]{1,0:T(8,128)S(1)} all-gather(f32[56,512]{1,0:T(8,128)S(1)} %concatenate.44), channel_id=3, replica_groups=mesh['date_0'=4,'date_1'=4,'date_2'=8,'band'=2] {'date_1'}, dimensions={0}, use_global_device_ids=true | all-gather | bytes 573440 | tf_op jit(solution)/shard_map/all_gather | solution.py:31
  82.2 10.1 %all-gather.2 = f32[224,512]{1,0:T(8,128)S(1)} all-gather(f32[56,512]{1,0:T(8,128)S(1)} %concatenate.45), channel_id=4, replica_groups=mesh['date_0'=4,'date_1'=4,'date_2'=8,'band'=2] {'date_0'}, dimensions={0}, use_global_device_ids=true | all-gather | bytes 573440 | tf_op jit(solution)/shard_map/all_gather | solution.py:31
  92.6 0.7 broadcast_in_dim.547
  93.3 15.3 %all-to-all-start = ((f32[2,4,18,512]{3,1,2,0:T(4,128)}), f32[2,4,18,512]{3,1,2,0:T(4,128)S(1)}, u32[]{:S(2)}, u32[]{:S(2)}) async-start(f32[2,4,18,512]{3,1,2,0:T(4,128)} %broadcast_in_dim.547), calls=%async_computation | async-start | bytes 589824 | tf_op jit(solution)/shard_map/all_to_all | solution.py:63
  108.9 0.9 all-to-all-done
  110.7 0.9 fusion.107
  112.2 3.6 %all-to-all-start.1 = ((f32[2,4,512]{2,1,0:T(4,128)}), f32[2,4,512]{2,1,0:T(4,128)S(1)}, u32[]{:S(2)}, u32[]{:S(2)}) async-start(f32[2,4,512]{2,1,0:T(4,128)} %broadcast_in_dim.565), calls=%async_computation.1 | async-start | bytes 32768 | tf_op jit(solution)/shard_map/all_to_all | solution.py:63
  116.4 0.9 copy.118
  (176 shorter events, 15.3 us)
Async XLA Ops:
  0.6 17.8 %copy-start.2 = (f32[64,4,512]{2,1,0:T(4,128)S(1)}, f32[64,4,512]{2,1,0:T(4,128)}, u32[]{:S(2)}) copy-start(f32[64,4,512]{2,1,0:T(4,128)} %param.5) | copy-start | bytes 1572868
  0.6 18.9 %copy-start.6 = (s32[64,512]{1,0:T(8,128)S(1)}, s32[64,512]{1,0:T(8,128)}, u32[]{:S(2)}) copy-start(s32[64,512]{1,0:T(8,128)} %param.6) | copy-start | bytes 393220
  20.2 7.6 %copy-start.3 = (f32[64,1,512]{2,1,0:T(1,128)S(1)}, f32[64,1,512]{2,1,0:T(1,128)}, u32[]{:S(2)}) copy-start(f32[64,1,512]{2,1,0:T(1,128)} %get-tuple-element.108) | copy-start | bytes 393220
  36.0 6.2 %copy-start.1 = (f32[5,64,512]{1,0,2:T(8,128)S(1)}, f32[5,64,512]{1,0,2:T(8,128)}, u32[]{:S(2)}) copy-start(f32[5,64,512]{1,0,2:T(8,128)} %get-tuple-element.104) | copy-start | bytes 1966084
  36.0 7.5 %copy-start = (f32[5,64,512]{1,0,2:T(8,128)S(1)}, f32[5,64,512]{1,0,2:T(8,128)}, u32[]{:S(2)}) copy-start(f32[5,64,512]{1,0,2:T(8,128)} %get-tuple-element.105) | copy-start | bytes 1966084
  39.0 5.8 %copy-start.18 = (f32[1,64]{1,0:T(1,128)S(1)}, f32[1,64]{1,0:T(1,128)}, u32[]{:S(2)}) copy-start(f32[1,64]{1,0:T(1,128)} %get-tuple-element.226) | copy-start | bytes 772
  39.1 5.8 %copy-start.19 = (f32[1,64]{1,0:T(1,128)S(1)}, f32[1,64]{1,0:T(1,128)}, u32[]{:S(2)}) copy-start(f32[1,64]{1,0:T(1,128)} %get-tuple-element.227) | copy-start | bytes 772
  39.1 5.8 %copy-start.20 = (f32[1,64]{1,0:T(1,128)S(1)}, f32[1,64]{1,0:T(1,128)}, u32[]{:S(2)}) copy-start(f32[1,64]{1,0:T(1,128)} %get-tuple-element.216) | copy-start | bytes 772
  39.1 5.8 %copy-start.21 = (f32[1,64]{1,0:T(1,128)S(1)}, f32[1,64]{1,0:T(1,128)}, u32[]{:S(2)}) copy-start(f32[1,64]{1,0:T(1,128)} %get-tuple-element.217) | copy-start | bytes 772
  39.1 5.8 %copy-start.22 = (f32[1,64]{1,0:T(1,128)S(1)}, f32[1,64]{1,0:T(1,128)}, u32[]{:S(2)}) copy-start(f32[1,64]{1,0:T(1,128)} %get-tuple-element.224) | copy-start | bytes 772
  39.1 5.8 %copy-start.23 = (f32[1,64]{1,0:T(1,128)S(1)}, f32[1,64]{1,0:T(1,128)}, u32[]{:S(2)}) copy-start(f32[1,64]{1,0:T(1,128)} %get-tuple-element.225) | copy-start | bytes 772
  39.1 5.8 %copy-start.24 = (f32[1,64]{1,0:T(1,128)S(1)}, f32[1,64]{1,0:T(1,128)}, u32[]{:S(2)}) copy-start(f32[1,64]{1,0:T(1,128)} %get-tuple-element.214) | copy-start | bytes 772
  39.1 5.8 %copy-start.25 = (f32[1,64]{1,0:T(1,128)S(1)}, f32[1,64]{1,0:T(1,128)}, u32[]{:S(2)}) copy-start(f32[1,64]{1,0:T(1,128)} %get-tuple-element.215) | copy-start | bytes 772
  39.1 5.8 %copy-start.26 = (f32[1,64]{1,0:T(1,128)S(1)}, f32[1,64]{1,0:T(1,128)}, u32[]{:S(2)}) copy-start(f32[1,64]{1,0:T(1,128)} %get-tuple-element.228) | copy-start | bytes 772
  39.1 5.8 %copy-start.27 = (f32[1,64]{1,0:T(1,128)S(1)}, f32[1,64]{1,0:T(1,128)}, u32[]{:S(2)}) copy-start(f32[1,64]{1,0:T(1,128)} %get-tuple-element.229) | copy-start | bytes 772
  39.1 5.8 %copy-start.28 = (f32[1,64]{1,0:T(1,128)S(1)}, f32[1,64]{1,0:T(1,128)}, u32[]{:S(2)}) copy-start(f32[1,64]{1,0:T(1,128)} %get-tuple-element.212) | copy-start | bytes 772
  39.2 5.8 %copy-start.29 = (f32[1,64]{1,0:T(1,128)S(1)}, f32[1,64]{1,0:T(1,128)}, u32[]{:S(2)}) copy-start(f32[1,64]{1,0:T(1,128)} %get-tuple-element.213) | copy-start | bytes 772
  39.2 5.8 %copy-start.30 = (f32[1,64]{1,0:T(1,128)S(1)}, f32[1,64]{1,0:T(1,128)}, u32[]{:S(2)}) copy-start(f32[1,64]{1,0:T(1,128)} %get-tuple-element.220) | copy-start | bytes 772
  39.2 5.8 %copy-start.31 = (f32[1,64]{1,0:T(1,128)S(1)}, f32[1,64]{1,0:T(1,128)}, u32[]{:S(2)}) copy-start(f32[1,64]{1,0:T(1,128)} %get-tuple-element.221) | copy-start | bytes 772
  39.2 5.8 %copy-start.32 = (f32[1,64]{1,0:T(1,128)S(1)}, f32[1,64]{1,0:T(1,128)}, u32[]{:S(2)}) copy-start(f32[1,64]{1,0:T(1,128)} %get-tuple-element.210) | copy-start | bytes 772
  39.2 5.8 %copy-start.33 = (f32[1,64]{1,0:T(1,128)S(1)}, f32[1,64]{1,0:T(1,128)}, u32[]{:S(2)}) copy-start(f32[1,64]{1,0:T(1,128)} %get-tuple-element.211) | copy-start | bytes 772
  39.2 5.8 %copy-start.34 = (f32[1,64]{1,0:T(1,128)S(1)}, f32[1,64]{1,0:T(1,128)}, u32[]{:S(2)}) copy-start(f32[1,64]{1,0:T(1,128)} %get-tuple-element.230) | copy-start | bytes 772
  39.2 5.8 %copy-start.35 = (f32[1,64]{1,0:T(1,128)S(1)}, f32[1,64]{1,0:T(1,128)}, u32[]{:S(2)}) copy-start(f32[1,64]{1,0:T(1,128)} %get-tuple-element.231) | copy-start | bytes 772
  39.2 5.8 %copy-start.36 = (f32[1,64]{1,0:T(1,128)S(1)}, f32[1,64]{1,0:T(1,128)}, u32[]{:S(2)}) copy-start(f32[1,64]{1,0:T(1,128)} %get-tuple-element.208) | copy-start | bytes 772
  39.2 5.8 %copy-start.37 = (f32[1,64]{1,0:T(1,128)S(1)}, f32[1,64]{1,0:T(1,128)}, u32[]{:S(2)}) copy-start(f32[1,64]{1,0:T(1,128)} %get-tuple-element.209) | copy-start | bytes 772
  39.2 5.8 %copy-start.38 = (f32[1,64]{1,0:T(1,128)S(1)}, f32[1,64]{1,0:T(1,128)}, u32[]{:S(2)}) copy-start(f32[1,64]{1,0:T(1,128)} %get-tuple-element.222) | copy-start | bytes 772
  39.3 5.8 %copy-start.39 = (f32[1,64]{1,0:T(1,128)S(1)}, f32[1,64]{1,0:T(1,128)}, u32[]{:S(2)}) copy-start(f32[1,64]{1,0:T(1,128)} %get-tuple-element.223) | copy-start | bytes 772
  39.3 5.8 %copy-start.40 = (f32[1,64]{1,0:T(1,128)S(1)}, f32[1,64]{1,0:T(1,128)}, u32[]{:S(2)}) copy-start(f32[1,64]{1,0:T(1,128)} %get-tuple-element.207) | copy-start | bytes 772
  39.3 5.8 %copy-start.41 = (f32[1,64]{1,0:T(1,128)S(1)}, f32[1,64]{1,0:T(1,128)}, u32[]{:S(2)}) copy-start(f32[1,64]{1,0:T(1,128)} %get-tuple-element.218) | copy-start | bytes 772
  93.3 16.5 %all-to-all-start = ((f32[2,4,18,512]{3,1,2,0:T(4,128)}), f32[2,4,18,512]{3,1,2,0:T(4,128)S(1)}, u32[]{:S(2)}, u32[]{:S(2)}) async-start(f32[2,4,18,512]{3,1,2,0:T(4,128)} %broadcast_in_dim.547), calls=%async_computation | async-start | bytes 589824 | tf_op jit(solution)/shard_map/all_to_all | solution.py:63
  110.7 6.7 %copy-start.8 = (pred[4,512]{1,0:T(4,128)(4,1)S(1)}, pred[4,512]{1,0:T(4,128)(4,1)}, u32[]{:S(2)}) copy-start(pred[4,512]{1,0:T(4,128)(4,1)} %get-tuple-element.89) | copy-start | bytes 6148
  112.2 5.2 %all-to-all-start.1 = ((f32[2,4,512]{2,1,0:T(4,128)}), f32[2,4,512]{2,1,0:T(4,128)S(1)}, u32[]{:S(2)}, u32[]{:S(2)}) async-start(f32[2,4,512]{2,1,0:T(4,128)} %broadcast_in_dim.565), calls=%async_computation.1 | async-start | bytes 32768 | tf_op jit(solution)/shard_map/all_to_all | solution.py:63
  (15 other events, 68.6 us)
where the time goes:
time: 120 us; the launch traced here: 118 us
  blocking collectives  44.8 us (37%)
  other arithmetic  26.1 us (22%)
  starting transfers between devices  18.9 us (16%)
  matrix products  15.4 us (13%)
  local copies, waits for them, and re-layouts  10.3 us (9%)
  between operations  1.64 us (1%)
    all_gather x3, blocking collectives, all_in_one(): both, at, found = (lax.all_gather(jnp.concatenate(lines), axis), 0, {})  44.8 us
    all_to_all x2, starting transfers between devices, sent_to_all(): lax.all_to_all(jnp.broadcast_to(value[None], (devices, *value.shape)), ax...  18.9 us
    mul x14, other arithmetic, window_pieces(): table = jnp.stack([design[i] * design[j] for i, j in upper_pairs])  8.64 us
    dot_general x4, matrix products, window_pieces(): jnp.einsum('rtp,it->rip', weight * series[:, b, :][None], design, precisi...  8.51 us
    reduce_sum x1, other arithmetic, window_pieces(): counts = jnp.sum(weight, axis=1)  5.54 us
    dot_general x1, matrix products, window_pieces(): sum_sq = jnp.einsum('rtp,tbp->rbp', weight, series * series, precision=hi)  5.54 us
    mul x4, local copies, waits for them, and re-layouts, window_pieces(): weight * series[:, b, :][None]  3.59 us
  transfers between devices with their start and end apart: 2, of which 1 were waited for; matrix products, arithmetic and copies ran while one was open for 2% of the time, Pallas kernels for 0%

commit v1 on v0

v1 whole, which is shorter than its diff:
```python
import functools
import math

import jax
import jax.numpy as jnp
from jax import lax
from jax.experimental import pallas as pl
from jax.experimental.pallas import tpu as pltpu
from jax.sharding import Mesh
from jax.sharding import PartitionSpec as P

DATE = ("date_0", "date_1", "date_2")
MESH = pl.DeviceIdType.MESH

GROUPS = (
    ((0, 0, 0), (1, 0, 0), (2, 0, 0), (0, 1, 0), (0, 2, 0), (0, 3, 0)),
    ((0, 1, 1), (0, 2, 1), (0, 3, 1), (0, 4, 0), (0, 5, 0), (0, 6, 0)),
    ((0, 4, 1), (0, 5, 1), (0, 6, 1), (1, 1, 0), (1, 2, 0), (1, 3, 0)),
    ((1, 1, 1), (1, 2, 1), (1, 3, 1)),
)
ROW_OF = {term: 8 * g + k for g, group in enumerate(GROUPS) for k, term in enumerate(group)}
DESIGN = ((0, 0, 0), (1, 0, 0), (0, 1, 0), (0, 1, 1), (0, 2, 0), (0, 2, 1), (0, 3, 0), (0, 3, 1))
SQ_ROW, FLAG_ROW = 6, 7


def split3(value):
    high = value.astype(jnp.bfloat16)
    rest = value - high.astype(jnp.float32)
    mid = rest.astype(jnp.bfloat16)
    low = (rest - mid.astype(jnp.float32)).astype(jnp.bfloat16)
    return high, mid, low


def table(terms, rows, first, dates, total):
    row = lax.broadcasted_iota(jnp.int32, (rows, 128), 0)
    lane = lax.broadcasted_iota(jnp.int32, (rows, 128), 1)
    t = (lax.rem(lane, dates) + first).astype(jnp.float32)
    power, harmonic, shift, there = (jnp.zeros((rows, 128), jnp.float32) for _ in range(4))
    for k, term in terms.items():
        here = row == k
        power = jnp.where(here, float(term[0]), power)
        harmonic = jnp.where(here, float(term[1]), harmonic)
        shift = jnp.where(here, float(term[2]), shift)
        there = jnp.where(here, 1.0, there)
    turn = 16.0 * harmonic * t - 1461.0 * shift
    turn = turn - 5844.0 * jnp.floor(turn * (1.0 / 5844.0) + 0.5)
    wave = jnp.cos(turn * (2.0 * math.pi / 5844.0))
    s = 2.0 * (t + 0.5) / total - 1.0
    scale = jnp.where(power > 0.5, s, 1.0) * jnp.where(power > 1.5, s, 1.0)
    return wave * scale * there


def kernel(
    sizes, total,
    obs, valid, breaks, refit, coef_out, spread_out,
    ov, vv, kv, hi_v, mid_v, lo_v, zsum, ebuf, zin, before, tot, lines, back, other, resid_v,
    in_sem, a_send, a_recv, b_send, b_recv, c_send, c_recv, x_send, x_recv, r_send, r_recv,
):
    ny, nx, nz = sizes
    nl = ny * nx
    nb, dates, px = ov.shape[0] // vv.shape[0], vv.shape[0], vv.shape[1]
    tiles = px // 128
    y, x, z = (lax.axis_index(a) for a in DATE)
    c = lax.axis_index("band")
    line = y * nx + x
    window = line * nz + z

    def along(d):
        return lax.rem(z + d, nz)

    def plane(d):
        p = lax.rem(line + d, nl)
        return (p // nx, lax.rem(p, nx), z, c)

    barrier = pltpu.get_barrier_semaphore()
    for d in range(1, nz):
        for core in (c, 1 - c):
            pl.semaphore_signal(
                barrier, inc=1, device_id=(y, x, along(d), core), device_id_type=MESH
            )
    pl.semaphore_signal(barrier, inc=1, device_id=(y, x, z, 1 - c), device_id_type=MESH)
    for d in range(1, nl):
        pl.semaphore_signal(barrier, inc=1, device_id=plane(d), device_id_type=MESH)

    loads = [
        pltpu.make_async_copy(breaks, kv, in_sem.at[0]),
        pltpu.make_async_copy(valid, vv, in_sem.at[1]),
    ]
    for b in range(nb):
        loads.append(
            pltpu.make_async_copy(
                obs.at[:, b, :], ov.at[pl.ds(b * dates, dates), :], in_sem.at[2 + b]
            )
        )
    for load in loads:
        load.start()

    first = window * dates
    basis = table({v: k for k, v in ROW_OF.items()}, 32, first, dates, float(total))
    design = table(dict(enumerate(DESIGN)), 8, first, dates, float(total))
    wide = jnp.concatenate([design] * (nb * dates // 128), axis=1)
    wide = jnp.concatenate([wide] * nb, axis=0)
    row = lax.broadcasted_iota(jnp.int32, wide.shape, 0)
    col = lax.broadcasted_iota(jnp.int32, wide.shape, 1)
    wide = jnp.where(row // 8 == col // dates, wide, 0.0)
    wide = jnp.concatenate(split3(wide), axis=0)
    basis = jnp.concatenate(split3(basis[:, :dates]), axis=0)

    picks = [refit[0, r] for r in range(4)]
    reach = lax.broadcasted_iota(jnp.int32, (8 + dates, dates), 0)
    tcol = lax.broadcasted_iota(jnp.int32, (8 + dates, dates), 1)
    upto = reach
    for r in range(4):
        upto = jnp.where(reach == dates + r, picks[r], upto)
    upto = jnp.where(tcol <= upto, 1.0, 0.0).astype(jnp.bfloat16)

    loads[0].wait()
    marks = jnp.dot(
        upto, kv[...].astype(jnp.float32).astype(jnp.bfloat16), preferred_element_type=jnp.float32
    )
    seg = marks[:dates]
    seg_at = marks[dates:]
    loads[1].wait()
    clear = vv[...].astype(jnp.float32)
    for load in loads[2:]:
        load.wait()
    series = ov[...]
    high, mid, low = split3(series)
    hi_v[...] = high
    mid_v[...] = mid
    lo_v[...] = low
    square = series * series
    square = functools.reduce(
        jnp.add, [square[b * dates : (b + 1) * dates] for b in range(nb)]
    )
    trow = lax.broadcasted_iota(jnp.int32, (dates, px), 0)
    n = 8 * nb

    def sums(r):
        inside = seg == seg_at[r : r + 1]
        if r < 4:
            inside = inside & (trow <= picks[r])
        weight = jnp.where(inside, clear, 0.0)
        narrow = weight.astype(jnp.bfloat16)
        tall = jnp.concatenate([narrow] * nb, axis=0)
        one = jnp.dot(wide, tall * hi_v[...], preferred_element_type=jnp.float32)
        two = jnp.dot(wide[: 2 * n], tall * mid_v[...], preferred_element_type=jnp.float32)
        three = jnp.dot(wide[:n], tall * lo_v[...], preferred_element_type=jnp.float32)
        moment = (one[2 * n :] + two[n:] + three) + (one[n : 2 * n] + two[:n]) + one[:n]
        gram = jnp.dot(basis, narrow, preferred_element_type=jnp.float32)
        gram = (gram[64:] + gram[32:64]) + gram[:32]
        sq = jnp.sum(weight * square, axis=0, keepdims=True)
        return moment, gram, sq

    moment, gram, sq = sums(4)
    mark = jnp.where(seg_at[4:5] > 0.5, 1.0, 0.0)
    row8 = lax.broadcasted_iota(jnp.int32, (8, px), 0)
    half = n // 2
    for h in range(2):
        extra = jnp.where(c == 0, gram[8 * h : 8 * h + 8], gram[16 + 8 * h : 24 + 8 * h])
        if h == 1:
            extra = jnp.where(row8 == SQ_ROW, sq, extra)
        extra = jnp.where(row8 == FLAG_ROW, mark, extra)
        for j in range(tiles):
            lanes = slice(128 * j, 128 * j + 128)
            ebuf[h * tiles + j, :half] = moment[half * h : half * h + half, lanes]
            ebuf[h * tiles + j, half:] = extra[:, lanes]

    pl.semaphore_wait(barrier, 2 * (nz - 1) + 1 + nl - 1)
    far_first = sorted(range(1, nz), key=lambda d: -min(d, nz - d))
    a_copies = []
    for d in far_first:
        p = along(d)
        copy = pltpu.make_async_remote_copy(
            src_ref=ebuf.at[p], dst_ref=zin.at[z], send_sem=a_send.at[d], recv_sem=a_recv.at[d],
            device_id=(y, x, p, c), device_id_type=MESH,
        )
        copy.start()
        a_copies.append(copy)
    zin[z] = ebuf[z]

    row32 = lax.broadcasted_iota(jnp.int32, (32, px), 0)
    opened = []
    for r in range(4):
        moment, gram, sq = sums(r)
        gram = jnp.where(row32 == 16 * c + 8 + SQ_ROW, sq, gram)
        opened.append(jnp.where(seg_at[r : r + 1] < 0.5, 1.0, 0.0))
        for j in range(tiles):
            lanes = slice(128 * j, 128 * j + 128)
            zsum[r * tiles + j, :32] = gram[:, lanes]
            zsum[r * tiles + j, 32:] = moment[:, lanes]

    for copy in a_copies:
        copy.wait()

    flag = half + FLAG_ROW

    def join(earlier, later):
        return earlier * (1.0 - later[flag : flag + 1]) + later

    acc = zin[0]
    before[0] = jnp.zeros_like(acc)
    for k in range(1, nz):
        before[k] = acc
        acc = join(acc, zin[k])
    tot[...] = acc
    lines[line] = acc
    b_copies = []
    far_first_l = sorted(
        range(1, nl), key=lambda d: -(min(d % nx, nx - d % nx) + min(d // nx, ny - d // nx))
    )
    for d in far_first_l:
        copy = pltpu.make_async_remote_copy(
            src_ref=tot, dst_ref=lines.at[line], send_sem=b_send.at[d], recv_sem=b_recv.at[d],
            device_id=plane(d), device_id_type=MESH,
        )
        copy.start()
        b_copies.append(copy)
    for copy in b_copies:
        copy.wait()
    acc = jnp.zeros_like(acc)
    for k in range(nl):
        acc = jnp.where(k < line, join(acc, lines[k]), acc)
    for k in range(nz):
        before[k] = join(acc, before[k])
    back[z] = before[z]
    c_copies = []
    for d in far_first:
        p = along(d)
        copy = pltpu.make_async_remote_copy(
            src_ref=before.at[p], dst_ref=back.at[z], send_sem=c_send.at[d], recv_sem=c_recv.at[d],
            device_id=(y, x, p, c), device_id_type=MESH,
        )
        copy.start()
        c_copies.append(copy)
        copy = pltpu.make_async_remote_copy(
            src_ref=before.at[p, pl.ds(half, 8)], dst_ref=other.at[z],
            send_sem=x_send.at[d], recv_sem=x_recv.at[d],
            device_id=(y, x, p, 1 - c), device_id_type=MESH,
        )
        copy.start()
        c_copies.append(copy)
    copy = pltpu.make_async_remote_copy(
        src_ref=before.at[z, pl.ds(half, 8)], dst_ref=other.at[z],
        send_sem=x_send.at[0], recv_sem=x_recv.at[0],
        device_id=(y, x, z, 1 - c), device_id_type=MESH,
    )
    copy.start()
    c_copies.append(copy)
    for copy in c_copies:
        copy.wait()

    for j in range(tiles):
        mine = [back[h * tiles + j, half:] for h in range(2)]
        theirs = [other[h * tiles + j] for h in range(2)]
        pieces = [jnp.where(c == 0, mine[h], theirs[h]) for h in range(2)]
        pieces += [jnp.where(c == 0, theirs[h], mine[h]) for h in range(2)]
        pieces += [back[h * tiles + j, :half] for h in range(2)]
        carried = jnp.concatenate(pieces, axis=0)
        for r in range(4):
            lanes = slice(128 * j, 128 * j + 128)
            zsum[r * tiles + j] = zsum[r * tiles + j] + opened[r][:, lanes] * carried

    def got(power, harmonic, shift):
        return zsum[:, ROW_OF[(power, harmonic, shift)], :]

    cosine = [got(0, k, 0) for k in range(7)]
    sine = [None] + [got(0, k, 1) for k in range(1, 7)]
    entry = [[None] * 8 for _ in range(8)]
    entry[0][0] = cosine[0]
    entry[1][0] = got(1, 0, 0)
    entry[1][1] = got(2, 0, 0)
    for k in range(1, 4):
        entry[2 * k][0] = cosine[k]
        entry[2 * k + 1][0] = sine[k]
        entry[2 * k][1] = got(1, k, 0)
        entry[2 * k + 1][1] = got(1, k, 1)
        for m in range(1, k + 1):
            entry[2 * k][2 * m] = 0.5 * (cosine[k - m] + cosine[k + m])
            entry[2 * k + 1][2 * m + 1] = 0.5 * (cosine[k - m] - cosine[k + m])
            if k == m:
                entry[2 * k + 1][2 * m] = 0.5 * sine[2 * k]
            else:
                entry[2 * k + 1][2 * m] = 0.5 * (sine[k + m] + sine[k - m])
                entry[2 * k][2 * m + 1] = 0.5 * (sine[k + m] - sine[k - m])
    lower = [[None] * 8 for _ in range(8)]
    inverse = [None] * 8
    for j in range(8):
        diag = entry[j][j] + 1.0
        for k in range(j):
            diag = diag - lower[j][k] * lower[j][k]
        root = lax.rsqrt(diag)
        root = root * (1.5 - 0.5 * diag * root * root)
        inverse[j] = root
        for i in range(j + 1, 8):
            value = entry[i][j]
            for k in range(j):
                value = value - lower[i][k] * lower[j][k]
            lower[i][j] = value * root
    resid = jnp.where(c == 0, zsum[:, 8 + SQ_ROW, :], zsum[:, 24 + SQ_ROW, :])
    for b in range(nb):
        rhs = [zsum[:, 32 + 8 * b + i, :] for i in range(8)]
        forward = []
        for i in range(8):
            value = rhs[i]
            for k in range(i):
                value = value - lower[i][k] * forward[k]
            forward.append(value * inverse[i])
        solved = [None] * 8
        for i in reversed(range(8)):
            value = forward[i]
            for k in range(i + 1, 8):
                value = value - lower[k][i] * solved[k]
            solved[i] = value * inverse[i]
        for i in range(8):
            resid = resid - solved[i] * (rhs[i] + solved[i])
            for r in range(4):
                coef_out[r, b, :, i, :] = solved[i][r * tiles : (r + 1) * tiles]
    resid_v[0] = resid
    copy = pltpu.make_async_remote_copy(
        src_ref=resid_v.at[0], dst_ref=resid_v.at[1], send_sem=r_send, recv_sem=r_recv,
        device_id=(y, x, z, 1 - c), device_id_type=MESH,
    )
    copy.start()
    copy.wait()
    spread_out[...] = (resid + resid_v[1]) / jnp.maximum(cosine[0], 1.0)


def per_device(sizes, observations, valid, breaks, refit):
    dates, nb, px = observations.shape
    ny, nx, nz = sizes
    tiles = px // 128
    assert nz == 2 * tiles
    f32, bf16 = jnp.float32, jnp.bfloat16
    chunk = 4 * nb + 8
    sem = pltpu.SemaphoreType.DMA
    coefs, spread = pl.pallas_call(
        functools.partial(kernel, sizes, dates * ny * nx * nz),
        out_shape=(
            jax.ShapeDtypeStruct((4, nb, tiles, 8, 128), f32),
            jax.ShapeDtypeStruct((4 * tiles, 128), f32),
        ),
        in_specs=[pl.BlockSpec(memory_space=pl.ANY)] * 3
        + [pl.BlockSpec(memory_space=pltpu.SMEM)],
        out_specs=(pl.BlockSpec(memory_space=pltpu.VMEM), pl.BlockSpec(memory_space=pltpu.VMEM)),
        scratch_shapes=[
            pltpu.VMEM((nb * dates, px), f32),
            pltpu.VMEM((dates, px), jnp.int32),
            pltpu.VMEM((dates, px), jnp.int32),
            pltpu.VMEM((nb * dates, px), bf16),
            pltpu.VMEM((nb * dates, px), bf16),
            pltpu.VMEM((nb * dates, px), bf16),
            pltpu.VMEM((4 * tiles, 32 + 8 * nb, 128), f32),
            pltpu.VMEM((nz, chunk, 128), f32),
            pltpu.VMEM((nz, chunk, 128), f32),
            pltpu.VMEM((nz, chunk, 128), f32),
            pltpu.VMEM((chunk, 128), f32),
            pltpu.VMEM((ny * nx, chunk, 128), f32),
            pltpu.VMEM((nz, chunk, 128), f32),
            pltpu.VMEM((nz, 8, 128), f32),
            pltpu.VMEM((2, 4 * tiles, 128), f32),
            sem((2 + nb,)),
            sem((nz,)), sem((nz,)),
            sem((ny * nx,)), sem((ny * nx,)),
            sem((nz,)), sem((nz,)),
            sem((nz,)), sem((nz,)),
            sem, sem,
        ],
        compiler_params=pltpu.CompilerParams(
            collective_id=0, has_side_effects=True, vmem_limit_bytes=32 * 1024 * 1024
        ),
    )(observations, valid, breaks, refit)
    coefs = jnp.transpose(coefs, (0, 1, 3, 2, 4)).reshape(1, 4, nb, 8, px)
    return coefs, spread.reshape(1, 4, px)


def solution(mesh):
    sizes = (4, 4, 8)
    split = Mesh(mesh.devices.reshape(*sizes, mesh.shape["band"]), (*DATE, "band"))
    placed = (P(DATE, "band", None), P(DATE, None), P(DATE, None), P(DATE, None))
    return jax.shard_map(
        functools.partial(per_device, sizes),
        mesh=split,
        in_specs=placed,
        out_specs=(P(DATE, None, "band", None, None), P(DATE, None, None)),
        check_vma=False,
    )
```

time: 120 us -> 37.1 us (0.31)
  the two profiles are of different devices: /device:TPU:25 before, /device:TPU:1 now
where the time goes in v1:
time: 37.1 us; the launch traced here: 36.9 us
  Pallas kernels  31.4 us (85%)
  local copies, waits for them, and re-layouts  4.81 us (13%)
  between operations  0.65 us (2%)
    pallas_call x1, Pallas kernels, per_device(): pl.pallas_call(functools.partial(kernel, sizes, dates * ny * nx * nz), ou...  31.4 us
    unnamed x9, local copies, waits for them, and re-layouts  4.2 us

profile of v1, /device:TPU:1, one launch (start us, length us, event | category | flops | bytes accessed | tf_op | source)
XLA Modules:
  0.0 36.9 jit_solution(10613103821767430604)
XLA Ops:
  0.6 0.0 copy-start
  0.6 1.0 %copy-done = f32[64,4,512]{2,1,0:T(4,128)S(1)} copy-done((f32[64,4,512]{2,1,0:T(4,128)S(1)}, f32[64,4,512]{2,1,0:T(4,128)}, u32[]{:S(2)}) %copy-start) | copy-done | bytes 524312
  1.7 0.0 copy-start.1
  1.7 0.9 %copy-done.1 = s32[64,512]{1,0:T(8,128)S(1)} copy-done((s32[64,512]{1,0:T(8,128)S(1)}, s32[64,512]{1,0:T(8,128)}, u32[]{:S(2)}) %copy-start.1) | copy-done | bytes 131096
  2.6 0.0 copy-start.2
  2.6 0.9 %copy-done.2 = s32[64,512]{1,0:T(8,128)S(1)} copy-done((s32[64,512]{1,0:T(8,128)S(1)}, s32[64,512]{1,0:T(8,128)}, u32[]{:S(2)}) %copy-start.2) | copy-done | bytes 131096
  3.5 0.0 copy-start.3
  3.5 0.7 %copy-done.3 = s32[1,4]{1,0:T(1,128)S(1)} copy-done((s32[1,4]{1,0:T(1,128)S(1)}, s32[1,4]{1,0:T(1,128)}, u32[]{:S(2)}) %copy-start.3) | copy-done | bytes 40
  4.1 31.4 %shard_map.59 = (f32[4,4,4,8,128]{4,3,2,1,0:T(8,128)S(1)}, f32[16,128]{1,0:T(8,128)S(1)}) custom-call(f32[64,4,512]{2,1,0:T(4,128)S(1)} %copy-done, s32[64,512]{1,0:T(8,128)S(1)} %copy-done.1, s32[64,512]{1,0:T(8,128)S(1)} %copy-done.2, s32[1,4]{1,0:T(1,128)S(1)} %copy-done.3), custom_call_target="tpu_custom_call" | custom-call | tf_op jit(solution)/shard_map/pallas_call | solution.py:337
  35.6 0.6 %reshape.11 = f32[1,4,512]{2,1,0:T(4,128)} reshape(f32[16,128]{1,0:T(8,128)S(1)} %get-tuple-element.5) | data formatting | bytes 16384 | tf_op jit(solution)/shard_map/reshape | solution.py:374
  36.2 0.7 %copy.7 = f32[1,4,4,8,512]{4,3,2,1,0:T(8,128)} copy(f32[1,4,4,8,512]{4,3,2,1,0:T(8,128)S(1)} %bitcast.3) | data formatting | bytes 524288
Async XLA Ops:
  0.6 1.0 %copy-start = (f32[64,4,512]{2,1,0:T(4,128)S(1)}, f32[64,4,512]{2,1,0:T(4,128)}, u32[]{:S(2)}) copy-start(f32[64,4,512]{2,1,0:T(4,128)} %obs.1) | copy-start | bytes 1572868
  1.7 0.9 %copy-start.1 = (s32[64,512]{1,0:T(8,128)S(1)}, s32[64,512]{1,0:T(8,128)}, u32[]{:S(2)}) copy-start(s32[64,512]{1,0:T(8,128)} %valid.1) | copy-start | bytes 393220
  2.6 0.9 %copy-start.2 = (s32[64,512]{1,0:T(8,128)S(1)}, s32[64,512]{1,0:T(8,128)}, u32[]{:S(2)}) copy-start(s32[64,512]{1,0:T(8,128)} %breaks.1) | copy-start | bytes 393220
  3.5 0.7 %copy-start.3 = (s32[1,4]{1,0:T(1,128)S(1)}, s32[1,4]{1,0:T(1,128)}, u32[]{:S(2)}) copy-start(s32[1,4]{1,0:T(1,128)} %refit.1) | copy-start | bytes 52

commit v2 on v1

--- a/solution.py
+++ b/solution.py
@@ -50,10 +50,10 @@
     return wave * scale * there
 
 
-def kernel(
+def sum_kernel(
     sizes, total,
-    obs, valid, breaks, refit, coef_out, spread_out,
-    ov, vv, kv, hi_v, mid_v, lo_v, zsum, ebuf, zin, before, tot, lines, back, other, resid_v,
+    obs, valid, breaks, refit, at_refit,
+    picked, ov, vv, kv, hi_v, mid_v, lo_v, zsum, theirs, ebuf, zin, before, tot, lines, back,
     in_sem, a_send, a_recv, b_send, b_recv, c_send, c_recv, x_send, x_recv, r_send, r_recv,
 ):
     ny, nx, nz = sizes
@@ -68,8 +68,7 @@
     def along(d):
         return lax.rem(z + d, nz)
 
-    def plane(d):
-        p = lax.rem(line + d, nl)
+    def at_line(p):
         return (p // nx, lax.rem(p, nx), z, c)
 
     barrier = pltpu.get_barrier_semaphore()
@@ -80,7 +79,10 @@
             )
     pl.semaphore_signal(barrier, inc=1, device_id=(y, x, z, 1 - c), device_id_type=MESH)
     for d in range(1, nl):
-        pl.semaphore_signal(barrier, inc=1, device_id=plane(d), device_id_type=MESH)
+
+        @pl.when(line >= d)
+        def _():
+            pl.semaphore_signal(barrier, inc=1, device_id=at_line(line - d), device_id_type=MESH)
 
     loads = [
         pltpu.make_async_copy(breaks, kv, in_sem.at[0]),
@@ -92,6 +94,8 @@
                 obs.at[:, b, :], ov.at[pl.ds(b * dates, dates), :], in_sem.at[2 + b]
             )
         )
+    pick_load = pltpu.make_async_copy(refit, picked, in_sem.at[2 + nb])
+    pick_load.start()
     for load in loads:
         load.start()
 
@@ -106,7 +110,8 @@
     wide = jnp.concatenate(split3(wide), axis=0)
     basis = jnp.concatenate(split3(basis[:, :dates]), axis=0)
 
-    picks = [refit[0, r] for r in range(4)]
+    pick_load.wait()
+    picks = [picked[:, r : r + 1] for r in range(4)]
     reach = lax.broadcasted_iota(jnp.int32, (8 + dates, dates), 0)
     tcol = lax.broadcasted_iota(jnp.int32, (8 + dates, dates), 1)
     upto = reach
@@ -166,7 +171,7 @@
             ebuf[h * tiles + j, :half] = moment[half * h : half * h + half, lanes]
             ebuf[h * tiles + j, half:] = extra[:, lanes]
 
-    pl.semaphore_wait(barrier, 2 * (nz - 1) + 1 + nl - 1)
+    pl.semaphore_wait(barrier, 2 * (nz - 1) + 1 + nl - 1 - line)
     far_first = sorted(range(1, nz), key=lambda d: -min(d, nz - d))
     a_copies = []
     for d in far_first:
@@ -179,16 +184,21 @@
         a_copies.append(copy)
     zin[z] = ebuf[z]
 
-    row32 = lax.broadcasted_iota(jnp.int32, (32, px), 0)
     opened = []
     for r in range(4):
         moment, gram, sq = sums(r)
-        gram = jnp.where(row32 == 16 * c + 8 + SQ_ROW, sq, gram)
+        square_row = jnp.where(row8 == SQ_ROW, sq, 0.0)
         opened.append(jnp.where(seg_at[r : r + 1] < 0.5, 1.0, 0.0))
         for j in range(tiles):
             lanes = slice(128 * j, 128 * j + 128)
-            zsum[r * tiles + j, :32] = gram[:, lanes]
-            zsum[r * tiles + j, 32:] = moment[:, lanes]
+            zsum[r * tiles + j, :n] = moment[:, lanes]
+            zsum[r * tiles + j, n : n + 8] = square_row[:, lanes]
+            zsum[r * tiles + j, n + 8 :] = gram[:, lanes]
+    swap = pltpu.make_async_remote_copy(
+        src_ref=zsum.at[:, pl.ds(0, n + 8)], dst_ref=theirs, send_sem=r_send, recv_sem=r_recv,
+        device_id=(y, x, z, 1 - c), device_id_type=MESH,
+    )
+    swap.start()
 
     for copy in a_copies:
         copy.wait()
@@ -205,64 +215,98 @@
         acc = join(acc, zin[k])
     tot[...] = acc
     lines[line] = acc
-    b_copies = []
-    far_first_l = sorted(
-        range(1, nl), key=lambda d: -(min(d % nx, nx - d % nx) + min(d // nx, ny - d // nx))
-    )
-    for d in far_first_l:
-        copy = pltpu.make_async_remote_copy(
+
+    def to_line(d):
+        return pltpu.make_async_remote_copy(
             src_ref=tot, dst_ref=lines.at[line], send_sem=b_send.at[d], recv_sem=b_recv.at[d],
-            device_id=plane(d), device_id_type=MESH,
+            device_id=at_line(line + d), device_id_type=MESH,
         )
-        copy.start()
-        b_copies.append(copy)
-    for copy in b_copies:
-        copy.wait()
+
+    def hops(d):
+        return min(d % nx, nx - d % nx) + min(d // nx, ny - d // nx)
+
+    for d in sorted(range(1, nl), key=lambda d: -hops(d)):
+
+        @pl.when(line + d < nl)
+        def _():
+            to_line(d).start()
+
+    for d in range(1, nl):
+
+        @pl.when(line >= d)
+        def _():
+            to_line(d).wait_recv()
+
     acc = jnp.zeros_like(acc)
     for k in range(nl):
         acc = jnp.where(k < line, join(acc, lines[k]), acc)
     for k in range(nz):
         before[k] = join(acc, before[k])
-    back[z] = before[z]
+    back[c, z] = before[z]
     c_copies = []
-    for d in far_first:
+    for d in [*far_first, 0]:
         p = along(d)
-        copy = pltpu.make_async_remote_copy(
-            src_ref=before.at[p], dst_ref=back.at[z], send_sem=c_send.at[d], recv_sem=c_recv.at[d],
-            device_id=(y, x, p, c), device_id_type=MESH,
-        )
-        copy.start()
-        c_copies.append(copy)
-        copy = pltpu.make_async_remote_copy(
-            src_ref=before.at[p, pl.ds(half, 8)], dst_ref=other.at[z],
-            send_sem=x_send.at[d], recv_sem=x_recv.at[d],
-            device_id=(y, x, p, 1 - c), device_id_type=MESH,
-        )
-        copy.start()
-        c_copies.append(copy)
-    copy = pltpu.make_async_remote_copy(
-        src_ref=before.at[z, pl.ds(half, 8)], dst_ref=other.at[z],
-        send_sem=x_send.at[0], recv_sem=x_recv.at[0],
-        device_id=(y, x, z, 1 - c), device_id_type=MESH,
-    )
-    copy.start()
-    c_copies.append(copy)
+        for core, send, recv in ((c, c_send, c_recv), (1 - c, x_send, x_recv)):
+            if d == 0 and core is c:
+                continue
+            copy = pltpu.make_async_remote_copy(
+                src_ref=before.at[p], dst_ref=back.at[c, z],
+                send_sem=send.at[d], recv_sem=recv.at[d],
+                device_id=(y, x, p, core), device_id_type=MESH,
+            )
+            copy.start()
+            c_copies.append(copy)
+    swap.wait()
     for copy in c_copies:
         copy.wait()
 
     for j in range(tiles):
-        mine = [back[h * tiles + j, half:] for h in range(2)]
-        theirs = [other[h * tiles + j] for h in range(2)]
-        pieces = [jnp.where(c == 0, mine[h], theirs[h]) for h in range(2)]
-        pieces += [jnp.where(c == 0, theirs[h], mine[h]) for h in range(2)]
-        pieces += [back[h * tiles + j, :half] for h in range(2)]
-        carried = jnp.concatenate(pieces, axis=0)
+        lanes = slice(128 * j, 128 * j + 128)
+        by_core = [[back[core, h * tiles + j] for h in range(2)] for core in range(2)]
+        pieces = []
+        for me in (0, 1):
+            moved = [jnp.where(c == me, by_core[0][h], by_core[1][h]) for h in range(2)]
+            pieces.append(
+                jnp.concatenate([moved[0][:half], moved[1][:half], moved[1][half:]], axis=0)
+            )
+        pieces.insert(1, jnp.concatenate([t[half:] for t in by_core[0] + by_core[1]], axis=0))
         for r in range(4):
-            lanes = slice(128 * j, 128 * j + 128)
-            zsum[r * tiles + j] = zsum[r * tiles + j] + opened[r][:, lanes] * carried
+            k = r * tiles + j
+            share = opened[r][:, lanes]
+            at_refit[k, : n + 8] = zsum[k, : n + 8] + share * pieces[0]
+            at_refit[k, n + 8 : n + 40] = zsum[k, n + 8 :] + share * pieces[1]
+            at_refit[k, n + 40 :] = theirs[k] + share * pieces[2]
+    for d in range(1, nl):
+
+        @pl.when(line + d < nl)
+        def _():
+            to_line(d).wait_send()
+
+
+def refit_kernel(at_refit, coef_out, spread_out, coef_v, spread_v, out_sem):
+    nb, tiles = coef_v.shape[1], coef_v.shape[2]
+    n = 8 * nb
+    rows = 8
+    each = rows // tiles
+    copies = []
+    for part in range(4 // each):
+        refit_part(at_refit, coef_v, spread_v, pl.ds(part * rows, rows), part * each, each)
+        there = pl.ds(part * each, each)
+        copy = pltpu.make_async_copy(coef_v.at[there], coef_out.at[there], out_sem.at[part])
+        copy.start()
+        copies.append(copy)
+    copy = pltpu.make_async_copy(spread_v, spread_out, out_sem.at[4 // each])
+    copy.start()
+    for copy in [*copies, copy]:
+        copy.wait()
+
+
+def refit_part(at_refit, coef_v, spread_v, lines, first, each):
+    nb, tiles = coef_v.shape[1], coef_v.shape[2]
+    n = 8 * nb
 
     def got(power, harmonic, shift):
-        return zsum[:, ROW_OF[(power, harmonic, shift)], :]
+        return at_refit[lines, n + 8 + ROW_OF[(power, harmonic, shift)], :]
 
     cosine = [got(0, k, 0) for k in range(7)]
     sine = [None] + [got(0, k, 1) for k in range(1, 7)]
@@ -283,47 +327,46 @@
             else:
                 entry[2 * k + 1][2 * m] = 0.5 * (sine[k + m] + sine[k - m])
                 entry[2 * k][2 * m + 1] = 0.5 * (sine[k + m] - sine[k - m])
-    lower = [[None] * 8 for _ in range(8)]
     inverse = [None] * 8
     for j in range(8):
-        diag = entry[j][j] + 1.0
-        for k in range(j):
-            diag = diag - lower[j][k] * lower[j][k]
+        diag = entry[j][j] + 1.0 if j == 0 else entry[j][j]
         root = lax.rsqrt(diag)
         root = root * (1.5 - 0.5 * diag * root * root)
         inverse[j] = root
         for i in range(j + 1, 8):
-            value = entry[i][j]
-            for k in range(j):
-                value = value - lower[i][k] * lower[j][k]
-            lower[i][j] = value * root
-    resid = jnp.where(c == 0, zsum[:, 8 + SQ_ROW, :], zsum[:, 24 + SQ_ROW, :])
-    for b in range(nb):
-        rhs = [zsum[:, 32 + 8 * b + i, :] for i in range(8)]
-        forward = []
-        for i in range(8):
-            value = rhs[i]
-            for k in range(i):
-                value = value - lower[i][k] * forward[k]
-            forward.append(value * inverse[i])
-        solved = [None] * 8
-        for i in reversed(range(8)):
-            value = forward[i]
-            for k in range(i + 1, 8):
-                value = value - lower[k][i] * solved[k]
-            solved[i] = value * inverse[i]
-        for i in range(8):
-            resid = resid - solved[i] * (rhs[i] + solved[i])
-            for r in range(4):
-                coef_out[r, b, :, i, :] = solved[i][r * tiles : (r + 1) * tiles]
-    resid_v[0] = resid
-    copy = pltpu.make_async_remote_copy(
-        src_ref=resid_v.at[0], dst_ref=resid_v.at[1], send_sem=r_send, recv_sem=r_recv,
-        device_id=(y, x, z, 1 - c), device_id_type=MESH,
-    )
-    copy.start()
-    copy.wait()
-    spread_out[...] = (resid + resid_v[1]) / jnp.maximum(cosine[0], 1.0)
+            entry[i][j] = entry[i][j] * root
+        for i in range(j + 1, 8):
+            for k in range(j + 1, i + 1):
+                value = entry[i][k]
+                if j == 0 and i == k:
+                    value = value + 1.0
+                entry[i][k] = value - entry[i][j] * entry[k][j]
+    resid = []
+    for mine, at in ((True, 0), (False, n + 40)):
+        total = at_refit[lines, at + n + SQ_ROW, :]
+        for b in range(nb):
+            rhs = [at_refit[lines, at + 8 * b + i, :] for i in range(8)]
+            work = list(rhs)
+            for i in range(8):
+                work[i] = work[i] * inverse[i]
+                for k in range(i + 1, 8):
+                    work[k] = work[k] - entry[k][i] * work[i]
+            for i in reversed(range(8)):
+                work[i] = work[i] * inverse[i]
+                for k in range(i):
+                    work[k] = work[k] - entry[i][k] * work[i]
+            terms = [work[i] * (rhs[i] + work[i]) for i in range(8)]
+            while len(terms) > 1:
+                terms = [p + q for p, q in zip(terms[::2], terms[1::2])]
+            total = total - terms[0]
+            if mine:
+                for i in range(8):
+                    for r in range(each):
+                        coef_v[first + r, b, :, i, :] = work[i][r * tiles : (r + 1) * tiles]
+        resid.append(total)
+    spread = (resid[0] + resid[1]) / jnp.maximum(cosine[0], 1.0)
+    for r in range(each):
+        spread_v[:, first + r, :] = spread[r * tiles : (r + 1) * tiles]
 
 
 def per_device(sizes, observations, valid, breaks, refit):
@@ -334,32 +377,29 @@
     f32, bf16 = jnp.float32, jnp.bfloat16
     chunk = 4 * nb + 8
     sem = pltpu.SemaphoreType.DMA
-    coefs, spread = pl.pallas_call(
-        functools.partial(kernel, sizes, dates * ny * nx * nz),
-        out_shape=(
-            jax.ShapeDtypeStruct((4, nb, tiles, 8, 128), f32),
-            jax.ShapeDtypeStruct((4 * tiles, 128), f32),
-        ),
-        in_specs=[pl.BlockSpec(memory_space=pl.ANY)] * 3
-        + [pl.BlockSpec(memory_space=pltpu.SMEM)],
-        out_specs=(pl.BlockSpec(memory_space=pltpu.VMEM), pl.BlockSpec(memory_space=pltpu.VMEM)),
+    args = (observations, valid, breaks, refit)
+    at_refit = pl.pallas_call(
+        functools.partial(sum_kernel, sizes, dates * ny * nx * nz),
+        out_shape=pltpu.VMEM((4 * tiles, 48 + 16 * nb, 128), f32),
+        in_specs=[pl.BlockSpec(memory_space=pltpu.HBM)] * 4,
+        out_specs=pl.BlockSpec(memory_space=pltpu.VMEM),
         scratch_shapes=[
+            pltpu.VMEM((1, 4), jnp.int32),
             pltpu.VMEM((nb * dates, px), f32),
             pltpu.VMEM((dates, px), jnp.int32),
             pltpu.VMEM((dates, px), jnp.int32),
             pltpu.VMEM((nb * dates, px), bf16),
             pltpu.VMEM((nb * dates, px), bf16),
             pltpu.VMEM((nb * dates, px), bf16),
-            pltpu.VMEM((4 * tiles, 32 + 8 * nb, 128), f32),
+            pltpu.VMEM((4 * tiles, 40 + 8 * nb, 128), f32),
+            pltpu.VMEM((4 * tiles, 8 + 8 * nb, 128), f32),
             pltpu.VMEM((nz, chunk, 128), f32),
             pltpu.VMEM((nz, chunk, 128), f32),
             pltpu.VMEM((nz, chunk, 128), f32),
             pltpu.VMEM((chunk, 128), f32),
             pltpu.VMEM((ny * nx, chunk, 128), f32),
-            pltpu.VMEM((nz, chunk, 128), f32),
-            pltpu.VMEM((nz, 8, 128), f32),
-            pltpu.VMEM((2, 4 * tiles, 128), f32),
-            sem((2 + nb,)),
+            pltpu.VMEM((2, nz, chunk, 128), f32),
+            sem((3 + nb,)),
             sem((nz,)), sem((nz,)),
             sem((ny * nx,)), sem((ny * nx,)),
             sem((nz,)), sem((nz,)),
@@ -367,11 +407,23 @@
             sem, sem,
         ],
         compiler_params=pltpu.CompilerParams(
-            collective_id=0, has_side_effects=True, vmem_limit_bytes=32 * 1024 * 1024
+            collective_id=0, has_side_effects=True, vmem_limit_bytes=24 * 1024 * 1024
         ),
-    )(observations, valid, breaks, refit)
+    )(*(pltpu.with_memory_space_constraint(a, pltpu.HBM) for a in args))
+    coefs, spread = pl.pallas_call(
+        refit_kernel,
+        out_shape=(pltpu.HBM((4, nb, tiles, 8, 128), f32), pltpu.HBM((tiles, 4, 128), f32)),
+        in_specs=[pl.BlockSpec(memory_space=pltpu.VMEM)],
+        out_specs=(pl.BlockSpec(memory_space=pltpu.HBM), pl.BlockSpec(memory_space=pltpu.HBM)),
+        scratch_shapes=[
+            pltpu.VMEM((4, nb, tiles, 8, 128), f32),
+            pltpu.VMEM((tiles, 4, 128), f32),
+            sem((3,)),
+        ],
+        compiler_params=pltpu.CompilerParams(vmem_limit_bytes=24 * 1024 * 1024),
+    )(pltpu.with_memory_space_constraint(at_refit, pltpu.VMEM))
     coefs = jnp.transpose(coefs, (0, 1, 3, 2, 4)).reshape(1, 4, nb, 8, px)
-    return coefs, spread.reshape(1, 4, px)
+    return coefs, jnp.transpose(spread, (1, 0, 2)).reshape(1, 4, px)
 
 
 def solution(mesh):

time: 37.1 us -> 29.4 us (0.79)
  the two profiles are of different devices: /device:TPU:1 before, /device:TPU:25 now
where the time goes in v2:
time: 29.4 us; the launch traced here: 29.3 us
  Pallas kernels  28.7 us (98%)
  between operations  0.64 us (2%)
    pallas_call x1, Pallas kernels, per_device(): pl.pallas_call(functools.partial(sum_kernel, sizes, dates * ny * nx * nz)...  24.7 us
    pallas_call x1, Pallas kernels, per_device(): pl.pallas_call(refit_kernel, out_shape=(pltpu.HBM((4, nb, tiles, 8, 128),...  3.97 us

profile of v2, /device:TPU:25, one launch (start us, length us, event | category | flops | bytes accessed | tf_op | source)
XLA Modules:
  0.0 29.3 jit_solution(12218849400801120609)
XLA Ops:
  0.6 24.7 %shard_map.59.at_refit = f32[16,112,128]{2,1,0:T(8,128)S(1)} custom-call(f32[64,4,512]{2,1,0:T(4,128)} %obs.1, s32[64,512]{1,0:T(8,128)} %valid.1, s32[64,512]{1,0:T(8,128)} %breaks.1, s32[1,4]{1,0:T(1,128)} %refit.1), custom_call_target="tpu_custom_call" | custom-call | tf_op jit(solution)/shard_map/pallas_call | solution.py:381
  25.4 4.0 %shard_map.60 = (f32[4,4,4,8,128]{4,3,2,1,0:T(8,128)}, f32[4,4,128]{2,1,0:T(4,128)}) custom-call(f32[16,112,128]{2,1,0:T(8,128)S(1)} %shard_map.59.at_refit), custom_call_target="tpu_custom_call" | custom-call | tf_op jit(solution)/shard_map/pallas_call | solution.py:413

commit v3 on v2

--- a/solution.py
+++ b/solution.py
@@ -273,9 +273,10 @@
         for r in range(4):
             k = r * tiles + j
             share = opened[r][:, lanes]
-            at_refit[k, : n + 8] = zsum[k, : n + 8] + share * pieces[0]
-            at_refit[k, n + 8 : n + 40] = zsum[k, n + 8 :] + share * pieces[1]
-            at_refit[k, n + 40 :] = theirs[k] + share * pieces[2]
+            at = k * (48 + 2 * n)
+            at_refit[at : at + n + 8] = zsum[k, : n + 8] + share * pieces[0]
+            at_refit[at + n + 8 : at + n + 40] = zsum[k, n + 8 :] + share * pieces[1]
+            at_refit[at + n + 40 : at + 2 * n + 48] = theirs[k] + share * pieces[2]
     for d in range(1, nl):
 
         @pl.when(line + d < nl)
@@ -283,15 +284,15 @@
             to_line(d).wait_send()
 
 
-def refit_kernel(at_refit, coef_out, spread_out, coef_v, spread_v, out_sem):
-    nb, tiles = coef_v.shape[1], coef_v.shape[2]
-    n = 8 * nb
+def refit_kernel(sizes, at_refit, coef_out, spread_out, coef_v, spread_v, out_sem):
+    nb, tiles = sizes
     rows = 8
     each = rows // tiles
+    span = nb * tiles * 8
     copies = []
     for part in range(4 // each):
-        refit_part(at_refit, coef_v, spread_v, pl.ds(part * rows, rows), part * each, each)
-        there = pl.ds(part * each, each)
+        refit_part(sizes, at_refit, coef_v, spread_v, part * rows, rows)
+        there = pl.ds(part * each * span, each * span)
         copy = pltpu.make_async_copy(coef_v.at[there], coef_out.at[there], out_sem.at[part])
         copy.start()
         copies.append(copy)
@@ -301,12 +302,17 @@
         copy.wait()
 
 
-def refit_part(at_refit, coef_v, spread_v, lines, first, each):
-    nb, tiles = coef_v.shape[1], coef_v.shape[2]
+def refit_part(sizes, at_refit, coef_v, spread_v, first, rows):
+    nb, tiles = sizes
     n = 8 * nb
+    each = rows // tiles
+    stride = 48 + 2 * n
+
+    def load(row):
+        return at_refit[pl.ds(first * stride + row, rows, stride=stride), :]
 
     def got(power, harmonic, shift):
-        return at_refit[lines, n + 8 + ROW_OF[(power, harmonic, shift)], :]
+        return load(n + 8 + ROW_OF[(power, harmonic, shift)])
 
     cosine = [got(0, k, 0) for k in range(7)]
     sine = [None] + [got(0, k, 1) for k in range(1, 7)]
@@ -343,9 +349,9 @@
                 entry[i][k] = value - entry[i][j] * entry[k][j]
     resid = []
     for mine, at in ((True, 0), (False, n + 40)):
-        total = at_refit[lines, at + n + SQ_ROW, :]
+        total = load(at + n + SQ_ROW)
         for b in range(nb):
-            rhs = [at_refit[lines, at + 8 * b + i, :] for i in range(8)]
+            rhs = [load(at + 8 * b + i) for i in range(8)]
             work = list(rhs)
             for i in range(8):
                 work[i] = work[i] * inverse[i]
@@ -362,11 +368,14 @@
             if mine:
                 for i in range(8):
                     for r in range(each):
-                        coef_v[first + r, b, :, i, :] = work[i][r * tiles : (r + 1) * tiles]
+                        at_coef = ((first // tiles + r) * nb + b) * tiles * 8 + i
+                        piece = work[i][r * tiles : (r + 1) * tiles]
+                        coef_v[pl.ds(at_coef, tiles, stride=8), :] = piece
         resid.append(total)
     spread = (resid[0] + resid[1]) / jnp.maximum(cosine[0], 1.0)
     for r in range(each):
-        spread_v[:, first + r, :] = spread[r * tiles : (r + 1) * tiles]
+        piece = spread[r * tiles : (r + 1) * tiles]
+        spread_v[pl.ds(first // tiles + r, tiles, stride=4), :] = piece
 
 
 def per_device(sizes, observations, valid, breaks, refit):
@@ -380,7 +389,7 @@
     args = (observations, valid, breaks, refit)
     at_refit = pl.pallas_call(
         functools.partial(sum_kernel, sizes, dates * ny * nx * nz),
-        out_shape=pltpu.VMEM((4 * tiles, 48 + 16 * nb, 128), f32),
+        out_shape=pltpu.VMEM((4 * tiles * (48 + 16 * nb), 128), f32),
         in_specs=[pl.BlockSpec(memory_space=pltpu.HBM)] * 4,
         out_specs=pl.BlockSpec(memory_space=pltpu.VMEM),
         scratch_shapes=[
@@ -411,19 +420,20 @@
         ),
     )(*(pltpu.with_memory_space_constraint(a, pltpu.HBM) for a in args))
     coefs, spread = pl.pallas_call(
-        refit_kernel,
-        out_shape=(pltpu.HBM((4, nb, tiles, 8, 128), f32), pltpu.HBM((tiles, 4, 128), f32)),
+        functools.partial(refit_kernel, (nb, tiles)),
+        out_shape=(pltpu.HBM((32 * nb * tiles, 128), f32), pltpu.HBM((4 * tiles, 128), f32)),
         in_specs=[pl.BlockSpec(memory_space=pltpu.VMEM)],
         out_specs=(pl.BlockSpec(memory_space=pltpu.HBM), pl.BlockSpec(memory_space=pltpu.HBM)),
         scratch_shapes=[
-            pltpu.VMEM((4, nb, tiles, 8, 128), f32),
-            pltpu.VMEM((tiles, 4, 128), f32),
+            pltpu.VMEM((32 * nb * tiles, 128), f32),
+            pltpu.VMEM((4 * tiles, 128), f32),
             sem((3,)),
         ],
         compiler_params=pltpu.CompilerParams(vmem_limit_bytes=24 * 1024 * 1024),
     )(pltpu.with_memory_space_constraint(at_refit, pltpu.VMEM))
-    coefs = jnp.transpose(coefs, (0, 1, 3, 2, 4)).reshape(1, 4, nb, 8, px)
-    return coefs, jnp.transpose(spread, (1, 0, 2)).reshape(1, 4, px)
+    coefs = jnp.transpose(coefs.reshape(4, nb, tiles, 8, 128), (0, 1, 3, 2, 4))
+    spread = jnp.transpose(spread.reshape(tiles, 4, 128), (1, 0, 2))
+    return coefs.reshape(1, 4, nb, 8, px), spread.reshape(1, 4, px)
 
 
 def solution(mesh):

time: 29.4 us -> 26.6 us (0.905)
  Pallas kernels: 28.7 us -> 25.9 us
    pallas_call x1, Pallas kernels: 3.97 us -> 1.17 us  [per_device(): pl.pallas_call(functools.partial(refit_kernel, (nb, tiles)), out_shape=(p...]
where the time goes in v3:
time: 26.6 us; the launch traced here: 26.5 us
  Pallas kernels  25.9 us (97%)
  between operations  0.64 us (2%)
    pallas_call x1, Pallas kernels, per_device(): pl.pallas_call(functools.partial(sum_kernel, sizes, dates * ny * nx * nz)...  24.7 us
    pallas_call x1, Pallas kernels, per_device(): pl.pallas_call(functools.partial(refit_kernel, (nb, tiles)), out_shape=(p...  1.17 us

profile of v3, /device:TPU:25, one launch (start us, length us, event | category | flops | bytes accessed | tf_op | source)
XLA Modules:
  0.0 26.5 jit_solution(634958672672929287)
XLA Ops:
  0.6 24.7 %shard_map.59.at_refit = f32[1792,128]{1,0:T(8,128)S(1)} custom-call(f32[64,4,512]{2,1,0:T(4,128)} %obs.1, s32[64,512]{1,0:T(8,128)} %valid.1, s32[64,512]{1,0:T(8,128)} %breaks.1, s32[1,4]{1,0:T(1,128)} %refit.1), custom_call_target="tpu_custom_call" | custom-call | tf_op jit(solution)/shard_map/pallas_call | solution.py:390
  25.4 1.2 %shard_map.60 = (f32[512,128]{1,0:T(8,128)}, f32[16,128]{1,0:T(8,128)}) custom-call(f32[1792,128]{1,0:T(8,128)S(1)} %shard_map.59.at_refit), custom_call_target="tpu_custom_call" | custom-call | tf_op jit(solution)/shard_map/pallas_call | solution.py:422

commit v4 on v3

--- a/solution.py
+++ b/solution.py
@@ -21,6 +21,8 @@
 ROW_OF = {term: 8 * g + k for g, group in enumerate(GROUPS) for k, term in enumerate(group)}
 DESIGN = ((0, 0, 0), (1, 0, 0), (0, 1, 0), (0, 1, 1), (0, 2, 0), (0, 2, 1), (0, 3, 0), (0, 3, 1))
 SQ_ROW, FLAG_ROW = 6, 7
+C_ORDER = (0, 1, 2, 3, 7, 6, 5, 4)
+B_ORDER = (6, 2, 10, 14, 1, 3, 5, 7, 9, 11, 13, 15, 4, 8, 12)
 
 
 def split3(value):
@@ -54,7 +56,7 @@
     sizes, total,
     obs, valid, breaks, refit, at_refit,
     picked, ov, vv, kv, hi_v, mid_v, lo_v, zsum, theirs, ebuf, zin, before, tot, lines, back,
-    in_sem, a_send, a_recv, b_send, b_recv, c_send, c_recv, x_send, x_recv, r_send, r_recv,
+    in_sem, a_send, a_recv, b_send, b_recv, c_send, c_recv, x_send, x_recv, r_send, r_recv, may_send,
 ):
     ny, nx, nz = sizes
     nl = ny * nx
@@ -71,18 +73,23 @@
     def at_line(p):
         return (p // nx, lax.rem(p, nx), z, c)
 
+    def rank(p):
+        across, down = lax.rem(p, nx), p // nx
+        across = jnp.minimum(across, nx - across)
+        return (2 * across + jnp.minimum(down, ny - down)) * nl + p
+
+    mine = rank(line)
+    others = [lax.rem(line + d, nl) for d in range(1, nl)]
+    lower = [(rank(p) < mine).astype(jnp.int32) for p in others]
+    later = [(p > line).astype(jnp.int32) for p in others]
+    greeted = sum(lower)
+    answers = sum((1 - low) * late for low, late in zip(lower, later))
+    far_first = sorted(range(1, nz), key=lambda d: -min(d, nz - d))
+
     barrier = pltpu.get_barrier_semaphore()
-    for d in range(1, nz):
-        for core in (c, 1 - c):
-            pl.semaphore_signal(
-                barrier, inc=1, device_id=(y, x, along(d), core), device_id_type=MESH
-            )
+    for d in far_first:
+        pl.semaphore_signal(barrier, inc=1, device_id=(y, x, along(d), c), device_id_type=MESH)
     pl.semaphore_signal(barrier, inc=1, device_id=(y, x, z, 1 - c), device_id_type=MESH)
-    for d in range(1, nl):
-
-        @pl.when(line >= d)
-        def _():
-            pl.semaphore_signal(barrier, inc=1, device_id=at_line(line - d), device_id_type=MESH)
 
     loads = [
         pltpu.make_async_copy(breaks, kv, in_sem.at[0]),
@@ -98,6 +105,11 @@
     pick_load.start()
     for load in loads:
         load.start()
+    for p, low in zip(others, lower):
+
+        @pl.when(low == 0)
+        def _():
+            pl.semaphore_signal(barrier, inc=1, device_id=at_line(p), device_id_type=MESH)
 
     first = window * dates
     basis = table({v: k for k, v in ROW_OF.items()}, 32, first, dates, float(total))
@@ -171,8 +183,7 @@
             ebuf[h * tiles + j, :half] = moment[half * h : half * h + half, lanes]
             ebuf[h * tiles + j, half:] = extra[:, lanes]
 
-    pl.semaphore_wait(barrier, 2 * (nz - 1) + 1 + nl - 1 - line)
-    far_first = sorted(range(1, nz), key=lambda d: -min(d, nz - d))
+    pl.semaphore_wait(barrier, nz + greeted)
     a_copies = []
     for d in far_first:
         p = along(d)
@@ -182,6 +193,12 @@
         )
         copy.start()
         a_copies.append(copy)
+    for p, low, late in zip(others, lower, later):
+
+        @pl.when((low == 1) & (late == 0))
+        def _():
+            pl.semaphore_signal(may_send, inc=1, device_id=at_line(p), device_id_type=MESH)
+
     zin[z] = ebuf[z]
 
     opened = []
@@ -222,10 +239,12 @@
             device_id=at_line(line + d), device_id_type=MESH,
         )
 
-    def hops(d):
-        return min(d % nx, nx - d % nx) + min(d // nx, ny - d // nx)
-
-    for d in sorted(range(1, nl), key=lambda d: -hops(d)):
+
+    @pl.when(answers > 0)
+    def _():
+        pl.semaphore_wait(may_send, answers)
+
+    for d in B_ORDER:
 
         @pl.when(line + d < nl)
         def _():
@@ -243,22 +262,27 @@
     for k in range(nz):
         before[k] = join(acc, before[k])
     back[c, z] = before[z]
-    c_copies = []
-    for d in [*far_first, 0]:
-        p = along(d)
-        for core, send, recv in ((c, c_send, c_recv), (1 - c, x_send, x_recv)):
-            if d == 0 and core is c:
-                continue
-            copy = pltpu.make_async_remote_copy(
-                src_ref=before.at[p], dst_ref=back.at[c, z],
-                send_sem=send.at[d], recv_sem=recv.at[d],
-                device_id=(y, x, p, core), device_id_type=MESH,
-            )
-            copy.start()
-            c_copies.append(copy)
+
+    def to_date(p, core, send, recv):
+        d = lax.rem(p - z + nz, nz)
+        return pltpu.make_async_remote_copy(
+            src_ref=before.at[p], dst_ref=back.at[c, z], send_sem=send.at[d], recv_sem=recv.at[d],
+            device_id=(y, x, p, core), device_id_type=MESH,
+        )
+
+    for p in C_ORDER:
+
+        @pl.when(p != z)
+        def _():
+            to_date(p, c, c_send, c_recv).start()
+
+        to_date(p, 1 - c, x_send, x_recv).start()
+
     swap.wait()
-    for copy in c_copies:
-        copy.wait()
+    for d in range(nz):
+        if d > 0:
+            to_date(along(d), c, c_send, c_recv).wait_recv()
+        to_date(along(d), 1 - c, x_send, x_recv).wait_recv()
 
     for j in range(tiles):
         lanes = slice(128 * j, 128 * j + 128)
@@ -282,6 +306,11 @@
         @pl.when(line + d < nl)
         def _():
             to_line(d).wait_send()
+
+    for d in range(1, nz):
+        to_date(along(d), c, c_send, c_recv).wait_send()
+    for p in range(nz):
+        to_date(p, 1 - c, x_send, x_recv).wait_send()
 
 
 def refit_kernel(sizes, at_refit, coef_out, spread_out, coef_v, spread_v, out_sem):
@@ -414,6 +443,7 @@
             sem((nz,)), sem((nz,)),
             sem((nz,)), sem((nz,)),
             sem, sem,
+            pltpu.SemaphoreType.REGULAR,
         ],
         compiler_params=pltpu.CompilerParams(
             collective_id=0, has_side_effects=True, vmem_limit_bytes=24 * 1024 * 1024

time: 26.6 us -> 25.8 us (0.970)
  Pallas kernels: 25.9 us -> 25 us
    pallas_call x1, Pallas kernels: 24.7 us -> 23.9 us  [per_device(): pl.pallas_call(functools.partial(sum_kernel, sizes, dates * ny * nx * nz)...]
where the time goes in v4:
time: 25.8 us; the launch traced here: 25.7 us
  Pallas kernels  25 us (97%)
  between operations  0.64 us (2%)
    pallas_call x1, Pallas kernels, per_device(): pl.pallas_call(functools.partial(sum_kernel, sizes, dates * ny * nx * nz)...  23.9 us
    pallas_call x1, Pallas kernels, per_device(): pl.pallas_call(functools.partial(refit_kernel, (nb, tiles)), out_shape=(p...  1.17 us

profile of v4, /device:TPU:25, one launch (start us, length us, event | category | flops | bytes accessed | tf_op | source)
XLA Modules:
  0.0 25.7 jit_solution(11880337748366437416)
XLA Ops:
  0.6 23.9 %shard_map.59.at_refit = f32[1792,128]{1,0:T(8,128)S(1)} custom-call(f32[64,4,512]{2,1,0:T(4,128)} %obs.1, s32[64,512]{1,0:T(8,128)} %valid.1, s32[64,512]{1,0:T(8,128)} %breaks.1, s32[1,4]{1,0:T(1,128)} %refit.1), custom_call_target="tpu_custom_call" | custom-call | tf_op jit(solution)/shard_map/pallas_call | solution.py:419
  24.5 1.2 %shard_map.60 = (f32[512,128]{1,0:T(8,128)}, f32[16,128]{1,0:T(8,128)}) custom-call(f32[1792,128]{1,0:T(8,128)S(1)} %shard_map.59.at_refit), custom_call_target="tpu_custom_call" | custom-call | tf_op jit(solution)/shard_map/pallas_call | solution.py:452

commit v5 on v4

--- a/solution.py
+++ b/solution.py
@@ -22,7 +22,6 @@
 DESIGN = ((0, 0, 0), (1, 0, 0), (0, 1, 0), (0, 1, 1), (0, 2, 0), (0, 2, 1), (0, 3, 0), (0, 3, 1))
 SQ_ROW, FLAG_ROW = 6, 7
 C_ORDER = (0, 1, 2, 3, 7, 6, 5, 4)
-B_ORDER = (6, 2, 10, 14, 1, 3, 5, 7, 9, 11, 13, 15, 4, 8, 12)
 
 
 def split3(value):
@@ -73,17 +72,6 @@
     def at_line(p):
         return (p // nx, lax.rem(p, nx), z, c)
 
-    def rank(p):
-        across, down = lax.rem(p, nx), p // nx
-        across = jnp.minimum(across, nx - across)
-        return (2 * across + jnp.minimum(down, ny - down)) * nl + p
-
-    mine = rank(line)
-    others = [lax.rem(line + d, nl) for d in range(1, nl)]
-    lower = [(rank(p) < mine).astype(jnp.int32) for p in others]
-    later = [(p > line).astype(jnp.int32) for p in others]
-    greeted = sum(lower)
-    answers = sum((1 - low) * late for low, late in zip(lower, later))
     far_first = sorted(range(1, nz), key=lambda d: -min(d, nz - d))
 
     barrier = pltpu.get_barrier_semaphore()
@@ -105,6 +93,18 @@
     pick_load.start()
     for load in loads:
         load.start()
+    def rank(p):
+        across, down = lax.rem(p, nx), p // nx
+        across = jnp.minimum(across, nx - across)
+        return (2 * across + jnp.minimum(down, ny - down)) * nl + p
+
+    mine = rank(line)
+    others = [lax.rem(line + d, nl) for d in range(1, nl)]
+    lower = [(rank(p) < mine).astype(jnp.int32) for p in others]
+    later = [(p > line).astype(jnp.int32) for p in others]
+    greeted = sum(lower)
+    answers = sum((1 - low) * late for low, late in zip(lower, later))
+
     for p, low in zip(others, lower):
 
         @pl.when(low == 0)
@@ -184,15 +184,16 @@
             ebuf[h * tiles + j, half:] = extra[:, lanes]
 
     pl.semaphore_wait(barrier, nz + greeted)
-    a_copies = []
-    for d in far_first:
+
+    def to_chunk(d):
         p = along(d)
-        copy = pltpu.make_async_remote_copy(
+        return pltpu.make_async_remote_copy(
             src_ref=ebuf.at[p], dst_ref=zin.at[z], send_sem=a_send.at[d], recv_sem=a_recv.at[d],
             device_id=(y, x, p, c), device_id_type=MESH,
         )
-        copy.start()
-        a_copies.append(copy)
+
+    for d in far_first:
+        to_chunk(d).start()
     for p, low, late in zip(others, lower, later):
 
         @pl.when((low == 1) & (late == 0))
@@ -217,21 +218,21 @@
     )
     swap.start()
 
-    for copy in a_copies:
-        copy.wait()
-
     flag = half + FLAG_ROW
 
     def join(earlier, later):
         return earlier * (1.0 - later[flag : flag + 1]) + later
 
-    acc = zin[0]
-    before[0] = jnp.zeros_like(acc)
-    for k in range(1, nz):
+    acc = jnp.zeros((half + 8, 128), jnp.float32)
+    for k in range(nz):
+
+        @pl.when(k != z)
+        def _():
+            to_chunk(lax.rem(z - k + nz, nz)).wait_recv()
+
         before[k] = acc
         acc = join(acc, zin[k])
     tot[...] = acc
-    lines[line] = acc
 
     def to_line(d):
         return pltpu.make_async_remote_copy(
@@ -244,21 +245,17 @@
     def _():
         pl.semaphore_wait(may_send, answers)
 
-    for d in B_ORDER:
-
-        @pl.when(line + d < nl)
-        def _():
-            to_line(d).start()
-
-    for d in range(1, nl):
-
-        @pl.when(line >= d)
-        def _():
-            to_line(d).wait_recv()
-
-    acc = jnp.zeros_like(acc)
-    for k in range(nl):
-        acc = jnp.where(k < line, join(acc, lines[k]), acc)
+    for p in sorted(range(1, nl), key=lambda p: (p % nx, -p)):
+
+        @pl.when(p > line)
+        def _():
+            to_line(p - line).start()
+
+    def fold(k, acc):
+        to_line(line - k).wait_recv()
+        return join(acc, lines[k])
+
+    acc = lax.fori_loop(0, line, fold, jnp.zeros_like(acc))
     for k in range(nz):
         before[k] = join(acc, before[k])
     back[c, z] = before[z]
@@ -279,13 +276,17 @@
         to_date(p, 1 - c, x_send, x_recv).start()
 
     swap.wait()
-    for d in range(nz):
-        if d > 0:
-            to_date(along(d), c, c_send, c_recv).wait_recv()
-        to_date(along(d), 1 - c, x_send, x_recv).wait_recv()
-
-    for j in range(tiles):
+    for j in reversed(range(tiles)):
         lanes = slice(128 * j, 128 * j + 128)
+        for q in (j, tiles + j):
+            p = along(lax.rem(z - q + nz, nz))
+
+            @pl.when(q != z)
+            def _():
+                to_date(p, c, c_send, c_recv).wait_recv()
+
+            to_date(p, 1 - c, x_send, x_recv).wait_recv()
+
         by_core = [[back[core, h * tiles + j] for h in range(2)] for core in range(2)]
         pieces = []
         for me in (0, 1):
@@ -308,6 +309,7 @@
             to_line(d).wait_send()
 
     for d in range(1, nz):
+        to_chunk(d).wait_send()
         to_date(along(d), c, c_send, c_recv).wait_send()
     for p in range(nz):
         to_date(p, 1 - c, x_send, x_recv).wait_send()

time: 25.8 us -> 25.4 us (0.984)
  Pallas kernels: 25 us -> 24.5 us
    pallas_call x1, Pallas kernels: 23.9 us -> 23.3 us  [per_device(): pl.pallas_call(functools.partial(sum_kernel, sizes, dates * ny * nx * nz)...]
where the time goes in v5:
time: 25.4 us; the launch traced here: 25.1 us
  Pallas kernels  24.5 us (96%)
  between operations  0.64 us (3%)
    pallas_call x1, Pallas kernels, per_device(): pl.pallas_call(functools.partial(sum_kernel, sizes, dates * ny * nx * nz)...  23.3 us
    pallas_call x1, Pallas kernels, per_device(): pl.pallas_call(functools.partial(refit_kernel, (nb, tiles)), out_shape=(p...  1.17 us

profile of v5, /device:TPU:25, one launch (start us, length us, event | category | flops | bytes accessed | tf_op | source)
XLA Modules:
  0.0 25.1 jit_solution(16985595019417333061)
XLA Ops:
  0.6 23.3 %shard_map.59.at_refit = f32[1792,128]{1,0:T(8,128)S(1)} custom-call(f32[64,4,512]{2,1,0:T(4,128)} %obs.1, s32[64,512]{1,0:T(8,128)} %valid.1, s32[64,512]{1,0:T(8,128)} %breaks.1, s32[1,4]{1,0:T(1,128)} %refit.1), custom_call_target="tpu_custom_call" | custom-call | tf_op jit(solution)/shard_map/pallas_call | solution.py:421
  24.0 1.2 %shard_map.60 = (f32[512,128]{1,0:T(8,128)}, f32[16,128]{1,0:T(8,128)}) custom-call(f32[1792,128]{1,0:T(8,128)S(1)} %shard_map.59.at_refit), custom_call_target="tpu_custom_call" | custom-call | tf_op jit(solution)/shard_map/pallas_call | solution.py:454

commit v6 on v5

--- a/solution.py
+++ b/solution.py
@@ -275,6 +275,18 @@
 
         to_date(p, 1 - c, x_send, x_recv).start()
 
+    for d in range(1, nl):
+
+        @pl.when(line + d < nl)
+        def _():
+            to_line(d).wait_send()
+
+    for d in range(1, nz):
+        to_chunk(d).wait_send()
+        to_date(along(d), c, c_send, c_recv).wait_send()
+    for p in range(nz):
+        to_date(p, 1 - c, x_send, x_recv).wait_send()
+
     swap.wait()
     for j in reversed(range(tiles)):
         lanes = slice(128 * j, 128 * j + 128)
@@ -302,17 +314,6 @@
             at_refit[at : at + n + 8] = zsum[k, : n + 8] + share * pieces[0]
             at_refit[at + n + 8 : at + n + 40] = zsum[k, n + 8 :] + share * pieces[1]
             at_refit[at + n + 40 : at + 2 * n + 48] = theirs[k] + share * pieces[2]
-    for d in range(1, nl):
-
-        @pl.when(line + d < nl)
-        def _():
-            to_line(d).wait_send()
-
-    for d in range(1, nz):
-        to_chunk(d).wait_send()
-        to_date(along(d), c, c_send, c_recv).wait_send()
-    for p in range(nz):
-        to_date(p, 1 - c, x_send, x_recv).wait_send()
 
 
 def refit_kernel(sizes, at_refit, coef_out, spread_out, coef_v, spread_v, out_sem):

time: 25.4 us -> 25.2 us (level)
  no operation moved by 1% of the time
where the time goes in v6:
time: 25.2 us; the launch traced here: 25 us
  Pallas kernels  24.4 us (97%)
  between operations  0.64 us (3%)
    pallas_call x1, Pallas kernels, per_device(): pl.pallas_call(functools.partial(sum_kernel, sizes, dates * ny * nx * nz)...  23.2 us
    pallas_call x1, Pallas kernels, per_device(): pl.pallas_call(functools.partial(refit_kernel, (nb, tiles)), out_shape=(p...  1.17 us

profile of v6, /device:TPU:25, one launch (start us, length us, event | category | flops | bytes accessed | tf_op | source)
XLA Modules:
  0.0 25.0 jit_solution(4580588650943433980)
XLA Ops:
  0.6 23.2 %shard_map.59.at_refit = f32[1792,128]{1,0:T(8,128)S(1)} custom-call(f32[64,4,512]{2,1,0:T(4,128)} %obs.1, s32[64,512]{1,0:T(8,128)} %valid.1, s32[64,512]{1,0:T(8,128)} %breaks.1, s32[1,4]{1,0:T(1,128)} %refit.1), custom_call_target="tpu_custom_call" | custom-call | tf_op jit(solution)/shard_map/pallas_call | solution.py:422
  23.9 1.2 %shard_map.60 = (f32[512,128]{1,0:T(8,128)}, f32[16,128]{1,0:T(8,128)}) custom-call(f32[1792,128]{1,0:T(8,128)S(1)} %shard_map.59.at_refit), custom_call_target="tpu_custom_call" | custom-call | tf_op jit(solution)/shard_map/pallas_call | solution.py:455

commit v7 on v6

--- a/solution.py
+++ b/solution.py
@@ -323,10 +323,9 @@
     span = nb * tiles * 8
     copies = []
     for part in range(4 // each):
-        refit_part(sizes, at_refit, coef_v, spread_v, part * rows, rows)
         there = pl.ds(part * each * span, each * span)
         copy = pltpu.make_async_copy(coef_v.at[there], coef_out.at[there], out_sem.at[part])
-        copy.start()
+        refit_part(sizes, at_refit, coef_v, spread_v, part * rows, rows, copy)
         copies.append(copy)
     copy = pltpu.make_async_copy(spread_v, spread_out, out_sem.at[4 // each])
     copy.start()
@@ -334,7 +333,7 @@
         copy.wait()
 
 
-def refit_part(sizes, at_refit, coef_v, spread_v, first, rows):
+def refit_part(sizes, at_refit, coef_v, spread_v, first, rows, copy):
     nb, tiles = sizes
     n = 8 * nb
     each = rows // tiles
@@ -404,6 +403,8 @@
                         piece = work[i][r * tiles : (r + 1) * tiles]
                         coef_v[pl.ds(at_coef, tiles, stride=8), :] = piece
         resid.append(total)
+        if mine:
+            copy.start()
     spread = (resid[0] + resid[1]) / jnp.maximum(cosine[0], 1.0)
     for r in range(each):
         piece = spread[r * tiles : (r + 1) * tiles]

time: 25.2 us -> 25.2 us (level)
  no operation moved by 1% of the time
where the time goes in v7:
time: 25.2 us; the launch traced here: 25 us
  Pallas kernels  24.4 us (97%)
  between operations  0.64 us (3%)
    pallas_call x1, Pallas kernels, per_device(): pl.pallas_call(functools.partial(sum_kernel, sizes, dates * ny * nx * nz)...  23.2 us
    pallas_call x1, Pallas kernels, per_device(): pl.pallas_call(functools.partial(refit_kernel, (nb, tiles)), out_shape=(p...  1.17 us

profile of v7, /device:TPU:25, one launch (start us, length us, event | category | flops | bytes accessed | tf_op | source)
XLA Modules:
  0.0 25.0 jit_solution(11550978488751760568)
XLA Ops:
  0.6 23.2 %shard_map.59.at_refit = f32[1792,128]{1,0:T(8,128)S(1)} custom-call(f32[64,4,512]{2,1,0:T(4,128)} %obs.1, s32[64,512]{1,0:T(8,128)} %valid.1, s32[64,512]{1,0:T(8,128)} %breaks.1, s32[1,4]{1,0:T(1,128)} %refit.1), custom_call_target="tpu_custom_call" | custom-call | tf_op jit(solution)/shard_map/pallas_call | solution.py:423
  23.9 1.2 %shard_map.60 = (f32[512,128]{1,0:T(8,128)}, f32[16,128]{1,0:T(8,128)}) custom-call(f32[1792,128]{1,0:T(8,128)S(1)} %shard_map.59.at_refit), custom_call_target="tpu_custom_call" | custom-call | tf_op jit(solution)/shard_map/pallas_call | solution.py:456
